TPU v7x, 32 devices: a whole 2x2x4 slice. The times are simulated.
32 devices in a mesh: src: 4 (over y, x), clip: 8 (over z, core).
Axes of the slice: x: 2, y: 2, z: 4, core: 2. Of those that a mesh axis runs over, the one named last changes fastest.
Arguments:
- color_masks: float32 [8, 2, 256, 256], P('clip', None, 'src'), may hold values from -1 to 1
- source_weights: float32 [4], P('src'), may hold values from 0.25 to 4
- pupil_shifts: int32 [4, 2], P('src'), may hold values from 0 to 16
- pupils: float32 [8, 2, 32, 32], replicated, may hold values from -6 to 6
- target_labels: int32 [8, 256, 256], P('clip'), may hold values from 0 to 2, as said below
Outputs:
- mask_grad: float32 [8, 2, 256, 256], P('clip', None, 'src')
- source_grad: float32 [4], P('src')
Inputs may be any that keep to these rules, and one draw needn't show every extreme that they name: `target_labels`: 0 marks an uncovered pixel, 1 and 2 the pixels of polygons of the first and of the second color.
All inputs are finite; a program needn't handle non-finite values.
Results may differ from a plain program's by a relative error of at most 0.0003.
Values sent between devices are 32-bit elements; how exact they have to be, the bound alone decides.
A program may use at most 64 MiB of HBM per device.

v0:
```python
import functools
import math

import jax
import jax.numpy as jnp
import ml_dtypes
import numpy as np
from jax import lax
from jax.experimental import pallas as pl
from jax.experimental.pallas import tpu as pltpu
from jax.sharding import PartitionSpec as P

K = 48
KP = 32
N = 2 * KP
LANES = 128
HALF = 64

steepness = 4.0
threshold = 0.6
loss_weight = 2.0
binarize = 0.25
f32 = jnp.float32
bf16 = jnp.bfloat16


def halves(table):
    high = table.astype(np.float32).astype(ml_dtypes.bfloat16)
    low = (table - high.astype(np.float64)).astype(np.float32).astype(ml_dtypes.bfloat16)
    return high, low


def beside(table):
    return np.concatenate(halves(table), axis=-1)


def above(table):
    return np.concatenate(halves(table), axis=-2)


def thrice(table):
    high, low = halves(table)
    return np.concatenate([high, low, high], axis=-1)


def spaced(real, imag):
    out = np.zeros((real.shape[0], LANES))
    out[:, : real.shape[1]] = real
    out[:, HALF : HALF + imag.shape[1]] = imag
    return out


def make_tables(height, src_devices):
    rows = height // src_devices
    pixels = np.arange(height)
    angles = 2.0 * np.pi * (((np.arange(K) - K // 2)[:, None] * pixels[None, :]) % height) / height
    scaling = 1.0 / math.sqrt(height * KP)
    fc, fs = np.cos(angles) * scaling, -np.sin(angles) * scaling
    coarse = np.arange(N)
    back = 2.0 * np.pi * ((coarse[:, None] * (np.arange(KP) - KP // 2)[None, :]) % N) / N
    bc, bs = np.cos(back), np.sin(back)
    band = np.arange(1, KP)
    step = height // N
    delta = (pixels[:, None] - step * coarse[None, :]) % height
    up = (1.0 + 2.0 * np.cos(2.0 * np.pi * ((delta[..., None] * band) % height) / height).sum(-1)) / N

    both = np.concatenate([fc, fs], axis=0)
    row_in = np.stack([thrice(both[:, s * rows : (s + 1) * rows]) for s in range(src_devices)])
    col_in = beside(np.concatenate([spaced(fc.T, fs.T), spaced(-fs.T, fc.T)], axis=0))
    half_in = np.zeros((LANES, LANES))
    half_in[:KP] = np.concatenate([bc.T, bs.T], axis=1)
    half_in[HALF : HALF + KP] = np.concatenate([-bs.T, bc.T], axis=1)
    half_in = beside(half_in)
    field_in = thrice(np.concatenate([bc, bs], axis=1))
    up_rows = thrice(up)
    zero = np.zeros_like(up)
    block = np.block([[up, zero], [zero, up]])
    up_cols = beside(block.T)
    down_cols = beside(block)
    down_rows = above(up.T)
    field_back = thrice(np.concatenate([bc.T, bs.T], axis=0))
    half_back = beside(np.concatenate([spaced(bc, -bs), spaced(bs, bc)], axis=0))
    col_back = np.zeros((LANES, 2 * height))
    col_back[:K] = np.concatenate([fc, -fs], axis=1)
    col_back[HALF : HALF + K] = np.concatenate([fs, fc], axis=1)
    col_back = beside(col_back)
    row_back = np.stack([above(both[:, s * rows : (s + 1) * rows].T) for s in range(src_devices)])
    return dict(
        row_in=row_in, col_in=col_in, half_in=half_in, field_in=field_in, up_rows=up_rows, up_cols=up_cols,
        down_cols=down_cols, down_rows=down_rows, field_back=field_back, half_back=half_back,
        col_back=col_back, row_back=row_back,
    )


ORDER = (
    "row_in", "col_in", "half_in", "field_in", "up_rows", "up_cols",
    "down_cols", "down_rows", "field_back", "half_back", "col_back", "row_back",
)
PER_SOURCE = ("row_in", "row_back")


def mm(left, right):
    return jnp.dot(left, right, preferred_element_type=f32)


def split(value):
    high = value.astype(bf16)
    return high, (value - high.astype(f32)).astype(bf16)


def times_table(value, table):
    high, low = split(value)
    width = table.shape[1] // 2
    first = mm(high, table[:, :width]) + mm(high, table[:, width:])
    return first + mm(low, table[:, :width])


def table_times(table, value):
    high, low = split(value)
    height = table.shape[0] // 2
    first = mm(table, high)
    return first[:height] + first[height:] + mm(table[:height], low)


def table_thrice(table, value):
    high, low = split(value)
    return mm(table, jnp.concatenate([high, high, low], axis=0))


def kernel(
    src_devices, clip_devices, scale,
    shifts, weights, masks_hbm, pupils_hbm, labels_hbm, *rest,
):
    count = len(ORDER)
    table_hbm = dict(zip(ORDER, rest[:count]))
    mask_out, term_out = rest[count : count + 2]
    tables = dict(zip(ORDER, rest[count + 2 : 2 * count + 2]))
    (
        masks, pupils, labels, pupil_real, pupil_imag, fields, padded, total,
        spec_slots, power_slots, grad_slots, term_slots,
        local_sems, spec_send, spec_recv, power_send, power_recv,
        grad_send, grad_recv, term_send, term_recv,
    ) = rest[2 * count + 2 :]
    me = lax.axis_index("src")
    my_clip = lax.axis_index("clip")

    def bring(name):
        source = table_hbm[name]
        if name in PER_SOURCE:
            source = source.at[me]
        return pltpu.make_async_copy(source, tables[name], local_sems.at[ORDER.index(name)])

    copy_masks = pltpu.make_async_copy(masks_hbm, masks, local_sems.at[count])
    copy_pupils = pltpu.make_async_copy(pupils_hbm, pupils, local_sems.at[count + 1])
    copy_labels = pltpu.make_async_copy(labels_hbm, labels, local_sems.at[count + 2])
    copies = {name: bring(name) for name in ORDER}
    copy_masks.start()
    copies["row_in"].start()
    copies["col_in"].start()
    copy_pupils.start()
    for name in ORDER[2:6]:
        copies[name].start()
    copy_labels.start()
    for name in ORDER[6:]:
        copies[name].start()

    barrier = pltpu.get_barrier_semaphore()
    for d in range(1, src_devices):
        pl.semaphore_signal(
            barrier, inc=1, device_id={"src": lax.rem(me + d, src_devices)}, device_id_type=pl.DeviceIdType.MESH
        )
    for d in range(1, clip_devices):
        pl.semaphore_signal(
            barrier, inc=1, device_id={"clip": lax.rem(my_clip + d, clip_devices)},
            device_id_type=pl.DeviceIdType.MESH,
        )

    def exchange(axis, devices, mine, slots, send, recv):
        sent = []
        for d in range(1, devices):
            copy = pltpu.make_async_remote_copy(
                src_ref=slots.at[mine], dst_ref=slots.at[mine],
                send_sem=send.at[d - 1], recv_sem=recv.at[d - 1],
                device_id={axis: lax.rem(mine + d, devices)}, device_id_type=pl.DeviceIdType.MESH,
            )
            copy.start()
            sent.append(copy)
        return sent

    def arrive(sent):
        for copy in sent:
            copy.wait_recv()

    def add_slots(slots, devices):
        value = slots[0]
        for d in range(1, devices):
            value = value + slots[d]
        return value

    lane = lax.broadcasted_iota(jnp.int32, (1, LANES), 1)
    low_half = lane < HALF
    sign = jnp.where(low_half, -1.0, 1.0).astype(f32)

    def rotate(value):
        return pltpu.roll(value, HALF, 1) * sign

    copy_masks.wait()
    copies["row_in"].wait()
    copies["col_in"].wait()
    height = masks.shape[2]
    both_masks = jnp.concatenate([masks[0], masks[1]], axis=1)
    rows_done = table_thrice(tables["row_in"][...], both_masks)
    stacked = jnp.concatenate(
        [
            jnp.concatenate([rows_done[:K, c * height : (c + 1) * height], rows_done[K:, c * height : (c + 1) * height]], axis=1)
            for c in range(2)
        ],
        axis=0,
    )
    spec_slots[me] = times_table(stacked, tables["col_in"][...])
    pl.semaphore_wait(barrier, src_devices + clip_devices - 2)
    spec_sent = exchange("src", src_devices, me, spec_slots, spec_send, spec_recv)

    copy_pupils.wait()
    channels = pupils.shape[0]
    blank = jnp.zeros((KP, HALF - KP), f32)
    for c in range(channels):
        pr, pi = pupils[c, 0], pupils[c, 1]
        pupil_real[c] = jnp.concatenate([pr, blank, pr, blank], axis=1)
        pupil_imag[c] = jnp.concatenate([pi, blank, pi, blank], axis=1)
    padded[...] = jnp.zeros_like(padded)
    first = shifts[0, 0]
    second = shifts[0, 1]
    weight = weights[0]
    copies["half_in"].wait()
    copies["field_in"].wait()

    arrive(spec_sent)
    total[...] = add_slots(spec_slots, src_devices)
    products = []
    for k in range(2):
        window = pltpu.roll(total[pl.ds(first + k * K, KP), :], lax.rem(LANES - second, LANES), 1)
        turned = rotate(window)
        for c in range(channels):
            products.append(pupil_real[c] * window + pupil_imag[c] * turned)
    half = times_table(jnp.concatenate(products, axis=0), tables["half_in"][...])
    half_high, half_low = split(half)
    turn_high, turn_low = split(rotate(half))
    columns = []
    for b in range(2 * channels):
        rows = slice(b * KP, (b + 1) * KP)
        columns.append(
            jnp.concatenate(
                [half_high[rows], turn_high[rows], half_high[rows], turn_high[rows], half_low[rows], turn_low[rows]],
                axis=0,
            )
        )
    power = []
    for k in range(2):
        wide = mm(tables["field_in"][...], jnp.concatenate(columns[k * channels : (k + 1) * channels], axis=1))
        fields[k] = wide
        squares = wide * wide
        summed = squares[:, :LANES]
        for c in range(1, channels):
            summed = summed + squares[:, c * LANES : (c + 1) * LANES]
        power.append(summed + pltpu.roll(summed, HALF, 1))
    raw = jnp.where(low_half, power[0], power[1]) * (1.0 / (channels * src_devices))
    power_slots[me] = raw * weight
    power_sent = exchange("src", src_devices, me, power_slots, power_send, power_recv)
    copies["up_rows"].wait()
    copies["up_cols"].wait()
    copy_labels.wait()
    for name in ORDER[6:]:
        copies[name].wait()
    arrive(power_sent)

    coarse = add_slots(power_slots, src_devices)
    tall = table_thrice(tables["up_rows"][...], coarse)
    chunk = HALF
    thin = []
    for r in range(0, height, chunk):
        intensity = times_table(tall[r : r + chunk], tables["up_cols"][...])
        resist = 1.0 / (1.0 + jnp.exp(-steepness * (intensity - threshold)))
        codes = labels[r : r + chunk, :]
        goal = jnp.concatenate([jnp.where(codes == 1, 1.0, 0.0), jnp.where(codes == 2, 1.0, 0.0)], axis=1).astype(f32)
        slope = (2.0 * loss_weight * steepness) * (resist - goal) * resist * (1.0 - resist)
        thin.append(times_table(slope, tables["down_cols"][...]))
    slope = table_times(tables["down_rows"][...], jnp.concatenate(thin, axis=0))

    term = jnp.sum(slope * raw, axis=0, keepdims=True)
    term_slots[my_clip] = jnp.broadcast_to(jnp.sum(term, axis=1, keepdims=True), (8, LANES))
    term_sent = exchange("clip", clip_devices, my_clip, term_slots, term_send, term_recv)

    slope = slope * (weight * (2.0 / (channels * src_devices)))
    swapped = pltpu.roll(slope, HALF, 1)
    doubled = [jnp.where(low_half, slope, swapped), jnp.where(low_half, swapped, slope)]
    pieces = []
    for k in range(2):
        field_grad = fields[k] * jnp.concatenate([doubled[k]] * channels, axis=1)
        back = table_thrice(tables["field_back"][...], field_grad)
        for c in range(channels):
            block = back[:, c * LANES : (c + 1) * LANES]
            pieces.append(block[:KP] - rotate(block[KP:]))
    product_grad = times_table(jnp.concatenate(pieces, axis=0), tables["half_back"][...])
    for k in range(2):
        along = jnp.zeros((KP, LANES), f32)
        across = jnp.zeros((KP, LANES), f32)
        for c in range(channels):
            b = k * channels + c
            block = product_grad[b * KP : (b + 1) * KP]
            along = along + pupil_real[c] * block
            across = across + pupil_imag[c] * block
        window_grad = along - rotate(across)
        padded[k, K - KP : K, :] = pltpu.roll(window_grad, second, 1)
    grad_slots[me] = jnp.concatenate([padded[k, pl.ds(K - KP - first, K), :] for k in range(2)], axis=0)
    grad_sent = exchange("src", src_devices, me, grad_slots, grad_send, grad_recv)

    arrive(term_sent)
    term_out[...] = add_slots(term_slots, clip_devices) * scale
    arrive(grad_sent)
    spread = times_table(add_slots(grad_slots, src_devices), tables["col_back"][...])
    width = 2 * height
    folded = jnp.concatenate(
        [
            jnp.concatenate([spread[:K, :height], spread[K:, :height]], axis=1),
            jnp.concatenate([spread[:K, height:width], spread[K:, height:width]], axis=1),
        ],
        axis=0,
    )
    grad = table_times(tables["row_back"][...], folded)
    mask_out[0] = grad[:, :height]
    mask_out[1] = grad[:, height:]
    for copy in spec_sent + power_sent + term_sent + grad_sent:
        copy.wait_send()


def per_device(color_masks, source_weights, pupil_shifts, pupils, target_labels):
    src_devices = lax.axis_size("src")
    clip_devices = lax.axis_size("clip")
    rows, height = color_masks.shape[2], color_masks.shape[3]
    channels = pupils.shape[0]
    tables = make_tables(height, src_devices)
    masks_here = color_masks[0]
    scale = src_devices / (2.0 * clip_devices * height * height)
    operands = [jnp.asarray(tables[name]) for name in ORDER]
    table_scratch = []
    for name in ORDER:
        shape = tables[name].shape[1:] if name in PER_SOURCE else tables[name].shape
        table_scratch.append(pltpu.VMEM(shape, bf16))
    smem = pl.BlockSpec(memory_space=pltpu.SMEM)
    far = pl.BlockSpec(memory_space=pl.ANY)
    near = pl.BlockSpec(memory_space=pltpu.VMEM)
    dma = pltpu.SemaphoreType.DMA
    mask_grad, terms = pl.pallas_call(
        functools.partial(kernel, src_devices, clip_devices, scale),
        out_shape=(
            jax.ShapeDtypeStruct((2, rows, height), f32),
            jax.ShapeDtypeStruct((8, LANES), f32),
        ),
        in_specs=[smem, smem] + [far] * (3 + len(ORDER)),
        out_specs=(near, near),
        scratch_shapes=table_scratch
        + [
            pltpu.VMEM((2, rows, height), f32),
            pltpu.VMEM(pupils.shape, f32),
            pltpu.VMEM((height, height), jnp.int32),
            pltpu.VMEM((channels, KP, LANES), f32),
            pltpu.VMEM((channels, KP, LANES), f32),
            pltpu.VMEM((2, N, channels * LANES), f32),
            pltpu.VMEM((2, 2 * K - KP, LANES), f32),
            pltpu.VMEM((2 * K, LANES), f32),
            pltpu.VMEM((src_devices, 2 * K, LANES), f32),
            pltpu.VMEM((src_devices, N, LANES), f32),
            pltpu.VMEM((src_devices, 2 * K, LANES), f32),
            pltpu.VMEM((clip_devices, 8, LANES), f32),
            dma((len(ORDER) + 3,)),
        ]
        + [dma((src_devices - 1,))] * 6
        + [dma((clip_devices - 1,))] * 2,
        compiler_params=pltpu.CompilerParams(
            collective_id=0, has_side_effects=True, vmem_limit_bytes=32 * 1024 * 1024
        ),
        name="abbe_gradient",
    )(pupil_shifts, source_weights, masks_here, pupils, target_labels[0], *operands)
    mask_grad = mask_grad - (4.0 * binarize) * (1.0 - masks_here * masks_here) * masks_here
    return mask_grad[None], terms[0, :1]


def solution(mesh):
    in_specs = (P("clip", None, "src", None), P("src"), P("src", None), P(), P("clip", None, None))
    out_specs = (P("clip", None, "src", None), P("src"))
    return jax.shard_map(
        per_device, mesh=mesh, in_specs=in_specs, out_specs=out_specs, check_vma=False
    )
```

profile of v0, /device:TPU:0, one launch (start us, length us, event | category | flops | bytes accessed | tf_op | source)
XLA Modules:
  0.0 39.6 jit_solution(694690728076956508)
XLA Ops:
  1.3 0.0 copy-start.15
  1.3 0.6 %copy-done.15 = s32[1,2]{1,0:T(1,128)S(1)} copy-done((s32[1,2]{1,0:T(1,128)S(1)}, s32[1,2]{1,0:T(1,128)}, u32[]{:S(2)}) %copy-start.15) | copy-done | bytes 32
  1.9 0.0 copy-start
  1.9 0.9 %copy-done = f32[1,2,64,256]{3,2,1,0:T(8,128)S(1)} copy-done((f32[1,2,64,256]{3,2,1,0:T(8,128)S(1)}, f32[1,2,64,256]{3,2,1,0:T(8,128)}, u32[]{:S(2)}) %copy-start) | copy-done | bytes 131096
  2.8 0.0 copy-start.1
  2.8 0.9 %copy-done.1 = f32[8,2,32,32]{3,2,1,0:T(8,128)S(1)} copy-done((f32[8,2,32,32]{3,2,1,0:T(8,128)S(1)}, f32[8,2,32,32]{3,2,1,0:T(8,128)}, u32[]{:S(2)}) %copy-start.1) | copy-done | bytes 65560
  3.8 0.0 copy-start.2
  3.8 0.9 %copy-done.2 = s32[1,256,256]{2,1,0:T(8,128)S(1)} copy-done((s32[1,256,256]{2,1,0:T(8,128)S(1)}, s32[1,256,256]{2,1,0:T(8,128)}, u32[]{:S(2)}) %copy-start.2) | copy-done | bytes 262168
  4.7 0.0 copy-start.3
  4.7 0.9 %copy-done.3 = bf16[128,1024]{1,0:T(8,128)(2,1)S(1)} copy-done((bf16[128,1024]{1,0:T(8,128)(2,1)S(1)}, bf16[128,1024]{1,0:T(8,128)(2,1)}, u32[]{:S(2)}) %copy-start.3) | copy-done | bytes 262168
  5.7 0.9 %copy-done.4 = bf16[512,256]{1,0:T(8,128)(2,1)S(1)} copy-done((bf16[512,256]{1,0:T(8,128)(2,1)S(1)}, bf16[512,256]{1,0:T(8,128)(2,1)}, u32[]{:S(2)}) %copy-start.4) | copy-done | bytes 262168
  6.6 0.9 %copy-done.5 = bf16[128,1024]{1,0:T(8,128)(2,1)S(1)} copy-done((bf16[128,1024]{1,0:T(8,128)(2,1)S(1)}, bf16[128,1024]{1,0:T(8,128)(2,1)}, u32[]{:S(2)}) %copy-start.5) | copy-done | bytes 262168
  7.6 0.9 %copy-done.6 = bf16[512,256]{1,0:T(8,128)(2,1)S(1)} copy-done((bf16[512,256]{1,0:T(8,128)(2,1)S(1)}, bf16[512,256]{1,0:T(8,128)(2,1)}, u32[]{:S(2)}) %copy-start.6) | copy-done | bytes 262168
  8.5 0.9 %copy-done.7 = bf16[4,96,192]{2,1,0:T(8,128)(2,1)S(1)} copy-done((bf16[4,96,192]{2,1,0:T(8,128)(2,1)S(1)}, bf16[4,96,192]{2,1,0:T(8,128)(2,1)}, u32[]{:S(2)}) %copy-start.7) | copy-done | bytes 147480
  9.5 0.9 %copy-done.8 = bf16[4,128,96]{2,1,0:T(8,128)(2,1)S(1)} copy-done((bf16[4,128,96]{2,1,0:T(8,128)(2,1)S(1)}, bf16[4,128,96]{2,1,0:T(8,128)(2,1)}, u32[]{:S(2)}) %copy-start.8) | copy-done | bytes 98328
  10.4 0.9 %copy-done.9 = bf16[256,192]{1,0:T(8,128)(2,1)S(1)} copy-done((bf16[256,192]{1,0:T(8,128)(2,1)S(1)}, bf16[256,192]{1,0:T(8,128)(2,1)}, u32[]{:S(2)}) %copy-start.9) | copy-done | bytes 98328
  11.3 0.8 %copy-done.10 = bf16[128,256]{1,0:T(8,128)(2,1)S(1)} copy-done((bf16[128,256]{1,0:T(8,128)(2,1)S(1)}, bf16[128,256]{1,0:T(8,128)(2,1)}, u32[]{:S(2)}) %copy-start.10) | copy-done | bytes 65560
  12.1 0.8 %copy-done.11 = bf16[128,256]{1,0:T(8,128)(2,1)S(1)} copy-done((bf16[128,256]{1,0:T(8,128)(2,1)S(1)}, bf16[128,256]{1,0:T(8,128)(2,1)}, u32[]{:S(2)}) %copy-start.11) | copy-done | bytes 65560
  13.0 0.8 %copy-done.12 = bf16[128,256]{1,0:T(8,128)(2,1)S(1)} copy-done((bf16[128,256]{1,0:T(8,128)(2,1)S(1)}, bf16[128,256]{1,0:T(8,128)(2,1)}, u32[]{:S(2)}) %copy-start.12) | copy-done | bytes 65560
  13.8 0.8 %copy-done.13 = bf16[64,192]{1,0:T(8,128)(2,1)S(1)} copy-done((bf16[64,192]{1,0:T(8,128)(2,1)S(1)}, bf16[64,192]{1,0:T(8,128)(2,1)}, u32[]{:S(2)}) %copy-start.13) | copy-done | bytes 24600
  14.6 0.8 %copy-done.14 = bf16[64,192]{1,0:T(8,128)(2,1)S(1)} copy-done((bf16[64,192]{1,0:T(8,128)(2,1)S(1)}, bf16[64,192]{1,0:T(8,128)(2,1)}, u32[]{:S(2)}) %copy-start.14) | copy-done | bytes 24600
  15.3 23.1 %abbe_gradient.1 = (f32[2,64,256]{2,1,0:T(8,128)S(1)}, f32[8,128]{1,0:T(8,128)S(1)}) custom-call(s32[1,2]{1,0:T(1,128)S(1)} %copy-done.15, f32[1]{0:T(128)S(6)} %copy.19.weights, f32[2,64,256]{2,1,0:T(8,128)S(1)} %bitcast.6, f32[8,2,32,32]{3,2,1,0:T(8,128)S(1)} %copy-done.1, s32[256,256]{1,0:T(8,128)S(1)} %bitcast.7, bf16[4,96,192]{2,1,0:T(8,128)(2,1)S(1)} %copy-done.7, ...), custom_call_target="tpu_custom_call" | custom-call | tf_op jit(solution)/shard_map/abbe_gradient/pallas_call | solution.py:354
  38.4 0.5 %slice.3 = f32[1,1]{1,0:T(1,128)} slice(f32[8,128]{1,0:T(8,128)S(1)} %get-tuple-element.5), slice={[0:1], [0:1]} | slice | bytes 8 | tf_op jit(solution)/shard_map/slice | solution.py:386
  38.9 0.7 %subtract_bitcast_fusion = f32[1,2,64,256]{3,2,1,0:T(8,128)} fusion(f32[2,64,256]{2,1,0:T(8,128)S(1)} %get-tuple-element.4, f32[1,2,64,256]{3,2,1,0:T(8,128)S(1)} %copy-done), kind=kLoop, calls=%fused_computation | loop fusion | flops 131072 | bytes 393216 | tf_op jit(solution)/shard_map/broadcast_in_dim | solution.py:386
  (11 shorter events, 0.0 us)
Async XLA Ops:
  1.3 0.7 %copy-start.15 = (s32[1,2]{1,0:T(1,128)S(1)}, s32[1,2]{1,0:T(1,128)}, u32[]{:S(2)}) copy-start(s32[1,2]{1,0:T(1,128)} %shifts.1) | copy-start | bytes 28
  1.9 0.9 %copy-start = (f32[1,2,64,256]{3,2,1,0:T(8,128)S(1)}, f32[1,2,64,256]{3,2,1,0:T(8,128)}, u32[]{:S(2)}) copy-start(f32[1,2,64,256]{3,2,1,0:T(8,128)} %param.17) | copy-start | bytes 393220
  2.8 0.9 %copy-start.1 = (f32[8,2,32,32]{3,2,1,0:T(8,128)S(1)}, f32[8,2,32,32]{3,2,1,0:T(8,128)}, u32[]{:S(2)}) copy-start(f32[8,2,32,32]{3,2,1,0:T(8,128)} %pupils_hbm.1) | copy-start | bytes 196612
  3.8 0.9 %copy-start.2 = (s32[1,256,256]{2,1,0:T(8,128)S(1)}, s32[1,256,256]{2,1,0:T(8,128)}, u32[]{:S(2)}) copy-start(s32[1,256,256]{2,1,0:T(8,128)} %param.21) | copy-start | bytes 786436
  4.7 0.9 %copy-start.3 = (bf16[128,1024]{1,0:T(8,128)(2,1)S(1)}, bf16[128,1024]{1,0:T(8,128)(2,1)}, u32[]{:S(2)}) copy-start(bf16[128,1024]{1,0:T(8,128)(2,1)} %constant.36.clone.rest_10_) | copy-start | bytes 786436
  5.7 0.9 %copy-start.4 = (bf16[512,256]{1,0:T(8,128)(2,1)S(1)}, bf16[512,256]{1,0:T(8,128)(2,1)}, u32[]{:S(2)}) copy-start(bf16[512,256]{1,0:T(8,128)(2,1)} %constant.32.clone.rest_6_) | copy-start | bytes 786436
  6.6 0.9 %copy-start.5 = (bf16[128,1024]{1,0:T(8,128)(2,1)S(1)}, bf16[128,1024]{1,0:T(8,128)(2,1)}, u32[]{:S(2)}) copy-start(bf16[128,1024]{1,0:T(8,128)(2,1)} %constant.31.clone.rest_5_) | copy-start | bytes 786436
  7.6 0.9 %copy-start.6 = (bf16[512,256]{1,0:T(8,128)(2,1)S(1)}, bf16[512,256]{1,0:T(8,128)(2,1)}, u32[]{:S(2)}) copy-start(bf16[512,256]{1,0:T(8,128)(2,1)} %constant.27.clone.rest_1_) | copy-start | bytes 786436
  8.5 0.9 %copy-start.7 = (bf16[4,96,192]{2,1,0:T(8,128)(2,1)S(1)}, bf16[4,96,192]{2,1,0:T(8,128)(2,1)}, u32[]{:S(2)}) copy-start(bf16[4,96,192]{2,1,0:T(8,128)(2,1)} %constant.26.clone.rest_0_) | copy-start | bytes 442372
  9.5 0.9 %copy-start.8 = (bf16[4,128,96]{2,1,0:T(8,128)(2,1)S(1)}, bf16[4,128,96]{2,1,0:T(8,128)(2,1)}, u32[]{:S(2)}) copy-start(bf16[4,128,96]{2,1,0:T(8,128)(2,1)} %constant.37.clone.rest_11_) | copy-start | bytes 294916
  10.4 0.9 %copy-start.9 = (bf16[256,192]{1,0:T(8,128)(2,1)S(1)}, bf16[256,192]{1,0:T(8,128)(2,1)}, u32[]{:S(2)}) copy-start(bf16[256,192]{1,0:T(8,128)(2,1)} %constant.30.clone.rest_4_) | copy-start | bytes 294916
  11.3 0.8 %copy-start.10 = (bf16[128,256]{1,0:T(8,128)(2,1)S(1)}, bf16[128,256]{1,0:T(8,128)(2,1)}, u32[]{:S(2)}) copy-start(bf16[128,256]{1,0:T(8,128)(2,1)} %constant.35.clone.rest_9_) | copy-start | bytes 196612
  12.1 0.8 %copy-start.11 = (bf16[128,256]{1,0:T(8,128)(2,1)S(1)}, bf16[128,256]{1,0:T(8,128)(2,1)}, u32[]{:S(2)}) copy-start(bf16[128,256]{1,0:T(8,128)(2,1)} %constant.33.clone.rest_7_) | copy-start | bytes 196612
  13.0 0.8 %copy-start.12 = (bf16[128,256]{1,0:T(8,128)(2,1)S(1)}, bf16[128,256]{1,0:T(8,128)(2,1)}, u32[]{:S(2)}) copy-start(bf16[128,256]{1,0:T(8,128)(2,1)} %constant.28.clone.rest_2_) | copy-start | bytes 196612
  13.8 0.8 %copy-start.13 = (bf16[64,192]{1,0:T(8,128)(2,1)S(1)}, bf16[64,192]{1,0:T(8,128)(2,1)}, u32[]{:S(2)}) copy-start(bf16[64,192]{1,0:T(8,128)(2,1)} %constant.34.clone.rest_8_) | copy-start | bytes 73732
  14.6 0.8 %copy-start.14 = (bf16[64,192]{1,0:T(8,128)(2,1)S(1)}, bf16[64,192]{1,0:T(8,128)(2,1)}, u32[]{:S(2)}) copy-start(bf16[64,192]{1,0:T(8,128)(2,1)} %constant.29.clone.rest_3_) | copy-start | bytes 73732
where the time goes:
time: 40.3 us; the launch traced here: 39.6 us
  Pallas kernels  23.1 us (57%)
  local copies, waits for them, and re-layouts  14.5 us (36%)
  between operations  1.31 us (3%)
  other arithmetic  0.68 us (2%)
    pallas_call x1, Pallas kernels, per_device(): pl.pallas_call(functools.partial(kernel, src_devices, clip_devices, scale...  23.1 us
    unnamed x32, local copies, waits for them, and re-layouts  14 us

commit v1 on v0

--- a/solution.py
+++ b/solution.py
@@ -15,6 +15,7 @@
 N = 2 * KP
 LANES = 128
 HALF = 64
+CHUNK = 64
 
 steepness = 4.0
 threshold = 0.6
@@ -73,10 +74,8 @@
     half_in = beside(half_in)
     field_in = thrice(np.concatenate([bc, bs], axis=1))
     up_rows = thrice(up)
-    zero = np.zeros_like(up)
-    block = np.block([[up, zero], [zero, up]])
-    up_cols = beside(block.T)
-    down_cols = beside(block)
+    up_cols = beside(np.concatenate([up.T, np.zeros_like(up.T)], axis=0))
+    down_cols = beside(np.concatenate([up, up], axis=1))
     down_rows = above(up.T)
     field_back = thrice(np.concatenate([bc.T, bs.T], axis=0))
     half_back = beside(np.concatenate([spaced(bc, -bs), spaced(bs, bc)], axis=0))
@@ -129,14 +128,14 @@
 
 def kernel(
     src_devices, clip_devices, scale,
-    shifts, weights, masks_hbm, pupils_hbm, labels_hbm, *rest,
+    shifts_hbm, weights_hbm, masks_hbm, pupils_hbm, labels_hbm, *rest,
 ):
     count = len(ORDER)
     table_hbm = dict(zip(ORDER, rest[:count]))
     mask_out, term_out = rest[count : count + 2]
     tables = dict(zip(ORDER, rest[count + 2 : 2 * count + 2]))
     (
-        masks, pupils, labels, pupil_real, pupil_imag, fields, padded, total,
+        shifts, weights, masks, pupils, labels, pupil_real, pupil_imag, fields, padded, total,
         spec_slots, power_slots, grad_slots, term_slots,
         local_sems, spec_send, spec_recv, power_send, power_recv,
         grad_send, grad_recv, term_send, term_recv,
@@ -153,11 +152,15 @@
     copy_masks = pltpu.make_async_copy(masks_hbm, masks, local_sems.at[count])
     copy_pupils = pltpu.make_async_copy(pupils_hbm, pupils, local_sems.at[count + 1])
     copy_labels = pltpu.make_async_copy(labels_hbm, labels, local_sems.at[count + 2])
+    copy_shifts = pltpu.make_async_copy(shifts_hbm, shifts, local_sems.at[count + 3])
+    copy_weights = pltpu.make_async_copy(weights_hbm, weights, local_sems.at[count + 4])
     copies = {name: bring(name) for name in ORDER}
     copy_masks.start()
     copies["row_in"].start()
     copies["col_in"].start()
     copy_pupils.start()
+    copy_shifts.start()
+    copy_weights.start()
     for name in ORDER[2:6]:
         copies[name].start()
     copy_labels.start()
@@ -208,18 +211,17 @@
     copies["row_in"].wait()
     copies["col_in"].wait()
     height = masks.shape[2]
-    both_masks = jnp.concatenate([masks[0], masks[1]], axis=1)
-    rows_done = table_thrice(tables["row_in"][...], both_masks)
-    stacked = jnp.concatenate(
-        [
-            jnp.concatenate([rows_done[:K, c * height : (c + 1) * height], rows_done[K:, c * height : (c + 1) * height]], axis=1)
-            for c in range(2)
-        ],
-        axis=0,
-    )
-    spec_slots[me] = times_table(stacked, tables["col_in"][...])
-    pl.semaphore_wait(barrier, src_devices + clip_devices - 2)
-    spec_sent = exchange("src", src_devices, me, spec_slots, spec_send, spec_recv)
+    colors = range(2)
+    spec_sent, power_sent, grad_sent = [], [], []
+    for k in colors:
+        rows_done = table_thrice(tables["row_in"][...], masks[k])
+        stacked = jnp.concatenate([rows_done[:K], rows_done[K:]], axis=1)
+        spec_slots[k, me] = times_table(stacked, tables["col_in"][...])
+        if k == 0:
+            pl.semaphore_wait(barrier, src_devices + clip_devices - 2)
+        spec_sent.append(
+            exchange("src", src_devices, me, spec_slots.at[k], spec_send.at[k], spec_recv.at[k])
+        )
 
     copy_pupils.wait()
     channels = pupils.shape[0]
@@ -229,109 +231,101 @@
         pupil_real[c] = jnp.concatenate([pr, blank, pr, blank], axis=1)
         pupil_imag[c] = jnp.concatenate([pi, blank, pi, blank], axis=1)
     padded[...] = jnp.zeros_like(padded)
+    copy_shifts.wait()
+    copy_weights.wait()
     first = shifts[0, 0]
     second = shifts[0, 1]
-    weight = weights[0]
+    weight = weights[0, 0]
     copies["half_in"].wait()
     copies["field_in"].wait()
 
-    arrive(spec_sent)
-    total[...] = add_slots(spec_slots, src_devices)
-    products = []
-    for k in range(2):
-        window = pltpu.roll(total[pl.ds(first + k * K, KP), :], lax.rem(LANES - second, LANES), 1)
+    raw = []
+    for k in colors:
+        arrive(spec_sent[k])
+        total[k] = add_slots(spec_slots.at[k], src_devices)
+        window = pltpu.roll(total[k, pl.ds(first, KP), :], lax.rem(LANES - second, LANES), 1)
         turned = rotate(window)
+        products = [pupil_real[c] * window + pupil_imag[c] * turned for c in range(channels)]
+        half = times_table(jnp.concatenate(products, axis=0), tables["half_in"][...])
+        half_high, half_low = split(half)
+        turn_high, turn_low = split(rotate(half))
+        columns = []
         for c in range(channels):
-            products.append(pupil_real[c] * window + pupil_imag[c] * turned)
-    half = times_table(jnp.concatenate(products, axis=0), tables["half_in"][...])
-    half_high, half_low = split(half)
-    turn_high, turn_low = split(rotate(half))
-    columns = []
-    for b in range(2 * channels):
-        rows = slice(b * KP, (b + 1) * KP)
-        columns.append(
-            jnp.concatenate(
-                [half_high[rows], turn_high[rows], half_high[rows], turn_high[rows], half_low[rows], turn_low[rows]],
-                axis=0,
+            rows = slice(c * KP, (c + 1) * KP)
+            columns.append(
+                jnp.concatenate(
+                    [half_high[rows], turn_high[rows], half_high[rows], turn_high[rows], half_low[rows], turn_low[rows]],
+                    axis=0,
+                )
             )
-        )
-    power = []
-    for k in range(2):
-        wide = mm(tables["field_in"][...], jnp.concatenate(columns[k * channels : (k + 1) * channels], axis=1))
+        wide = mm(tables["field_in"][...], jnp.concatenate(columns, axis=1))
         fields[k] = wide
         squares = wide * wide
         summed = squares[:, :LANES]
         for c in range(1, channels):
             summed = summed + squares[:, c * LANES : (c + 1) * LANES]
-        power.append(summed + pltpu.roll(summed, HALF, 1))
-    raw = jnp.where(low_half, power[0], power[1]) * (1.0 / (channels * src_devices))
-    power_slots[me] = raw * weight
-    power_sent = exchange("src", src_devices, me, power_slots, power_send, power_recv)
+        power = (summed + pltpu.roll(summed, HALF, 1)) * (1.0 / (channels * src_devices))
+        raw.append(power)
+        power_slots[k, me] = jnp.where(low_half, power[: N // 2], power[N // 2 :]) * weight
+        power_sent.append(
+            exchange("src", src_devices, me, power_slots.at[k], power_send.at[k], power_recv.at[k])
+        )
     copies["up_rows"].wait()
     copies["up_cols"].wait()
     copy_labels.wait()
     for name in ORDER[6:]:
         copies[name].wait()
-    arrive(power_sent)
-
-    coarse = add_slots(power_slots, src_devices)
-    tall = table_thrice(tables["up_rows"][...], coarse)
-    chunk = HALF
-    thin = []
-    for r in range(0, height, chunk):
-        intensity = times_table(tall[r : r + chunk], tables["up_cols"][...])
-        resist = 1.0 / (1.0 + jnp.exp(-steepness * (intensity - threshold)))
-        codes = labels[r : r + chunk, :]
-        goal = jnp.concatenate([jnp.where(codes == 1, 1.0, 0.0), jnp.where(codes == 2, 1.0, 0.0)], axis=1).astype(f32)
-        slope = (2.0 * loss_weight * steepness) * (resist - goal) * resist * (1.0 - resist)
-        thin.append(times_table(slope, tables["down_cols"][...]))
-    slope = table_times(tables["down_rows"][...], jnp.concatenate(thin, axis=0))
-
-    term = jnp.sum(slope * raw, axis=0, keepdims=True)
-    term_slots[my_clip] = jnp.broadcast_to(jnp.sum(term, axis=1, keepdims=True), (8, LANES))
-    term_sent = exchange("clip", clip_devices, my_clip, term_slots, term_send, term_recv)
-
-    slope = slope * (weight * (2.0 / (channels * src_devices)))
-    swapped = pltpu.roll(slope, HALF, 1)
-    doubled = [jnp.where(low_half, slope, swapped), jnp.where(low_half, swapped, slope)]
-    pieces = []
-    for k in range(2):
-        field_grad = fields[k] * jnp.concatenate([doubled[k]] * channels, axis=1)
+
+    term = jnp.zeros((1, LANES), f32)
+    for k in colors:
+        arrive(power_sent[k])
+        packed = add_slots(power_slots.at[k], src_devices)
+        coarse = jnp.concatenate([packed, pltpu.roll(packed, HALF, 1)], axis=0)
+        tall = table_thrice(tables["up_rows"][...], coarse)
+        thin = []
+        for r in range(0, height, CHUNK):
+            intensity = times_table(tall[r : r + CHUNK], tables["up_cols"][...])
+            level = jnp.tanh((0.5 * steepness) * (intensity - threshold))
+            shifted = level + jnp.where(labels[r : r + CHUNK, :] == k + 1, -1.0, 1.0)
+            slope = (0.25 * loss_weight * steepness) * shifted * (1.0 - level * level)
+            thin.append(times_table(slope, tables["down_cols"][...]))
+        slope = table_times(tables["down_rows"][...], jnp.concatenate(thin, axis=0))
+        term = term + jnp.sum(slope * raw[k], axis=0, keepdims=True)
+        if k == 1:
+            term_slots[my_clip] = jnp.broadcast_to(0.5 * jnp.sum(term, axis=1, keepdims=True), (8, LANES))
+            term_sent = exchange("clip", clip_devices, my_clip, term_slots, term_send, term_recv)
+
+        slope = slope * (weight * (2.0 / (channels * src_devices)))
+        field_grad = fields[k] * jnp.concatenate([slope] * channels, axis=1)
         back = table_thrice(tables["field_back"][...], field_grad)
+        pieces = []
         for c in range(channels):
             block = back[:, c * LANES : (c + 1) * LANES]
             pieces.append(block[:KP] - rotate(block[KP:]))
-    product_grad = times_table(jnp.concatenate(pieces, axis=0), tables["half_back"][...])
-    for k in range(2):
+        product_grad = times_table(jnp.concatenate(pieces, axis=0), tables["half_back"][...])
         along = jnp.zeros((KP, LANES), f32)
         across = jnp.zeros((KP, LANES), f32)
         for c in range(channels):
-            b = k * channels + c
-            block = product_grad[b * KP : (b + 1) * KP]
+            block = product_grad[c * KP : (c + 1) * KP]
             along = along + pupil_real[c] * block
             across = across + pupil_imag[c] * block
         window_grad = along - rotate(across)
         padded[k, K - KP : K, :] = pltpu.roll(window_grad, second, 1)
-    grad_slots[me] = jnp.concatenate([padded[k, pl.ds(K - KP - first, K), :] for k in range(2)], axis=0)
-    grad_sent = exchange("src", src_devices, me, grad_slots, grad_send, grad_recv)
-
+        grad_slots[k, me] = padded[k, pl.ds(K - KP - first, K), :]
+        grad_sent.append(
+            exchange("src", src_devices, me, grad_slots.at[k], grad_send.at[k], grad_recv.at[k])
+        )
+
+    for k in colors:
+        arrive(grad_sent[k])
+        spread = times_table(add_slots(grad_slots.at[k], src_devices), tables["col_back"][...])
+        folded = jnp.concatenate([spread[:, :height], spread[:, height:]], axis=0)
+        mask_out[k] = table_times(tables["row_back"][...], folded)
     arrive(term_sent)
     term_out[...] = add_slots(term_slots, clip_devices) * scale
-    arrive(grad_sent)
-    spread = times_table(add_slots(grad_slots, src_devices), tables["col_back"][...])
-    width = 2 * height
-    folded = jnp.concatenate(
-        [
-            jnp.concatenate([spread[:K, :height], spread[K:, :height]], axis=1),
-            jnp.concatenate([spread[:K, height:width], spread[K:, height:width]], axis=1),
-        ],
-        axis=0,
-    )
-    grad = table_times(tables["row_back"][...], folded)
-    mask_out[0] = grad[:, :height]
-    mask_out[1] = grad[:, height:]
-    for copy in spec_sent + power_sent + term_sent + grad_sent:
-        copy.wait_send()
+    for sent in spec_sent + power_sent + [term_sent] + grad_sent:
+        for copy in sent:
+            copy.wait_send()
 
 
 def per_device(color_masks, source_weights, pupil_shifts, pupils, target_labels):
@@ -347,8 +341,7 @@
     for name in ORDER:
         shape = tables[name].shape[1:] if name in PER_SOURCE else tables[name].shape
         table_scratch.append(pltpu.VMEM(shape, bf16))
-    smem = pl.BlockSpec(memory_space=pltpu.SMEM)
-    far = pl.BlockSpec(memory_space=pl.ANY)
+    far = pl.BlockSpec(memory_space=pltpu.HBM)
     near = pl.BlockSpec(memory_space=pltpu.VMEM)
     dma = pltpu.SemaphoreType.DMA
     mask_grad, terms = pl.pallas_call(
@@ -357,10 +350,12 @@
             jax.ShapeDtypeStruct((2, rows, height), f32),
             jax.ShapeDtypeStruct((8, LANES), f32),
         ),
-        in_specs=[smem, smem] + [far] * (3 + len(ORDER)),
+        in_specs=[far] * (5 + len(ORDER)),
         out_specs=(near, near),
         scratch_shapes=table_scratch
         + [
+            pltpu.SMEM((1, 2), jnp.int32),
+            pltpu.SMEM((1, 1), f32),
             pltpu.VMEM((2, rows, height), f32),
             pltpu.VMEM(pupils.shape, f32),
             pltpu.VMEM((height, height), jnp.int32),
@@ -368,20 +363,20 @@
             pltpu.VMEM((channels, KP, LANES), f32),
             pltpu.VMEM((2, N, channels * LANES), f32),
             pltpu.VMEM((2, 2 * K - KP, LANES), f32),
-            pltpu.VMEM((2 * K, LANES), f32),
-            pltpu.VMEM((src_devices, 2 * K, LANES), f32),
-            pltpu.VMEM((src_devices, N, LANES), f32),
-            pltpu.VMEM((src_devices, 2 * K, LANES), f32),
+            pltpu.VMEM((2, K, LANES), f32),
+            pltpu.VMEM((2, src_devices, K, LANES), f32),
+            pltpu.VMEM((2, src_devices, N // 2, LANES), f32),
+            pltpu.VMEM((2, src_devices, K, LANES), f32),
             pltpu.VMEM((clip_devices, 8, LANES), f32),
-            dma((len(ORDER) + 3,)),
+            dma((len(ORDER) + 5,)),
         ]
-        + [dma((src_devices - 1,))] * 6
+        + [dma((2, src_devices - 1))] * 6
         + [dma((clip_devices - 1,))] * 2,
         compiler_params=pltpu.CompilerParams(
-            collective_id=0, has_side_effects=True, vmem_limit_bytes=32 * 1024 * 1024
+            collective_id=0, has_side_effects=True, vmem_limit_bytes=60 * 1024 * 1024
         ),
         name="abbe_gradient",
-    )(pupil_shifts, source_weights, masks_here, pupils, target_labels[0], *operands)
+    )(pupil_shifts, source_weights[None], masks_here, pupils, target_labels[0], *operands)
     mask_grad = mask_grad - (4.0 * binarize) * (1.0 - masks_here * masks_here) * masks_here
     return mask_grad[None], terms[0, :1]
 

time: 40.3 us -> 26.2 us (0.65); the launches traced: 39.6 us -> 26 us
  local copies, waits for them, and re-layouts: 14.5 us -> 1.19 us
  Pallas kernels: 23.1 us -> 21.9 us
  other arithmetic: 0.68 us -> 1.58 us
    unnamed x32 -> x2, local copies, waits for them, and re-layouts: 14 us -> 0.01 us
    pallas_call x1, Pallas kernels: 23.1 us -> 21.9 us  [per_device(): pl.pallas_call(functools.partial(kernel, src_devices, clip_devices, scale...]
    broadcast_in_dim x1, other arithmetic: 0.68 us -> 1.58 us  [per_device(): return (mask_grad[None], terms[0, :1])]
    slice x1, local copies, waits for them, and re-layouts: 0.51 us -> 1.18 us  [per_device(): return (mask_grad[None], terms[0, :1])]
where the time goes in v1:
time: 26.2 us; the launch traced here: 26 us
  Pallas kernels  21.9 us (84%)
  other arithmetic  1.58 us (6%)
  between operations  1.29 us (5%)
  local copies, waits for them, and re-layouts  1.19 us (5%)
    pallas_call x1, Pallas kernels, per_device(): pl.pallas_call(functools.partial(kernel, src_devices, clip_devices, scale...  21.9 us
    broadcast_in_dim x1, other arithmetic, per_device(): return (mask_grad[None], terms[0, :1])  1.58 us
    slice x1, local copies, waits for them, and re-layouts, per_device(): return (mask_grad[None], terms[0, :1])  1.18 us

profile of v1, /device:TPU:0, one launch (start us, length us, event | category | flops | bytes accessed | tf_op | source)
XLA Modules:
  0.0 26.0 jit_solution(15349328781685921158)
XLA Ops:
  1.3 0.0 copy-start
  1.3 21.9 %abbe_gradient.1 = (f32[2,64,256]{2,1,0:T(8,128)}, f32[8,128]{1,0:T(8,128)}) custom-call(s32[1,2]{1,0:T(1,128)} %shifts_hbm.1, f32[1,1]{1,0:T(1,128)} %bitcast.7.weights_hbm, f32[2,64,256]{2,1,0:T(8,128)} %bitcast.8, f32[8,2,32,32]{3,2,1,0:T(8,128)} %pupils_hbm.1, s32[256,256]{1,0:T(8,128)} %bitcast.9, bf16[4,96,192]{2,1,0:T(8,128)(2,1)} %constant.26.clone.rest_0_, ...), custom_call_target="tpu_custom_call" | custom-call | tf_op jit(solution)/shard_map/abbe_gradient/pallas_call | solution.py:347
  23.2 1.2 %slice.3 = f32[1,1]{1,0:T(1,128)} slice(f32[8,128]{1,0:T(8,128)} %get-tuple-element.5), slice={[0:1], [0:1]} | slice | bytes 8 | tf_op jit(solution)/shard_map/slice | solution.py:381
  24.4 0.0 copy-done
  24.4 1.6 %subtract_bitcast_fusion = f32[1,2,64,256]{3,2,1,0:T(8,128)} fusion(f32[2,64,256]{2,1,0:T(8,128)} %get-tuple-element.4, f32[1,2,64,256]{3,2,1,0:T(8,128)S(1)} %copy-done), kind=kLoop, calls=%fused_computation | loop fusion | flops 131072 | bytes 393216 | tf_op jit(solution)/shard_map/broadcast_in_dim | solution.py:381
Async XLA Ops:
  1.3 23.1 %copy-start = (f32[1,2,64,256]{3,2,1,0:T(8,128)S(1)}, f32[1,2,64,256]{3,2,1,0:T(8,128)}, u32[]{:S(2)}) copy-start(f32[1,2,64,256]{3,2,1,0:T(8,128)} %param.17) | copy-start | bytes 393220

commit v2 on v1

--- a/solution.py
+++ b/solution.py
@@ -138,10 +138,21 @@
         shifts, weights, masks, pupils, labels, pupil_real, pupil_imag, fields, padded, total,
         spec_slots, power_slots, grad_slots, term_slots,
         local_sems, spec_send, spec_recv, power_send, power_recv,
-        grad_send, grad_recv, term_send, term_recv,
+        grad_send, grad_recv, term_send, term_recv, result, term_result, out_sems,
     ) = rest[2 * count + 2 :]
     me = lax.axis_index("src")
     my_clip = lax.axis_index("clip")
+
+    barrier = pltpu.get_barrier_semaphore()
+    for d in range(1, src_devices):
+        pl.semaphore_signal(
+            barrier, inc=1, device_id={"src": lax.rem(me + d, src_devices)}, device_id_type=pl.DeviceIdType.MESH
+        )
+    for d in range(1, clip_devices):
+        pl.semaphore_signal(
+            barrier, inc=1, device_id={"clip": lax.rem(my_clip + d, clip_devices)},
+            device_id_type=pl.DeviceIdType.MESH,
+        )
 
     def bring(name):
         source = table_hbm[name]
@@ -167,17 +178,6 @@
     for name in ORDER[6:]:
         copies[name].start()
 
-    barrier = pltpu.get_barrier_semaphore()
-    for d in range(1, src_devices):
-        pl.semaphore_signal(
-            barrier, inc=1, device_id={"src": lax.rem(me + d, src_devices)}, device_id_type=pl.DeviceIdType.MESH
-        )
-    for d in range(1, clip_devices):
-        pl.semaphore_signal(
-            barrier, inc=1, device_id={"clip": lax.rem(my_clip + d, clip_devices)},
-            device_id_type=pl.DeviceIdType.MESH,
-        )
-
     def exchange(axis, devices, mine, slots, send, recv):
         sent = []
         for d in range(1, devices):
@@ -235,7 +235,7 @@
     copy_weights.wait()
     first = shifts[0, 0]
     second = shifts[0, 1]
-    weight = weights[0, 0]
+    weight = weights[0]
     copies["half_in"].wait()
     copies["field_in"].wait()
 
@@ -316,16 +316,38 @@
             exchange("src", src_devices, me, grad_slots.at[k], grad_send.at[k], grad_recv.at[k])
         )
 
+    leaving = []
     for k in colors:
         arrive(grad_sent[k])
         spread = times_table(add_slots(grad_slots.at[k], src_devices), tables["col_back"][...])
         folded = jnp.concatenate([spread[:, :height], spread[:, height:]], axis=0)
-        mask_out[k] = table_times(tables["row_back"][...], folded)
-    arrive(term_sent)
-    term_out[...] = add_slots(term_slots, clip_devices) * scale
+        plane = masks[k]
+        pull = (4.0 * binarize) * (1.0 - plane * plane) * plane
+        result[k] = table_times(tables["row_back"][...], folded) - pull
+        leaving.append(pltpu.make_async_copy(result.at[k], mask_out.at[k], out_sems.at[k]))
+        leaving[-1].start()
+        if k == 0:
+            arrive(term_sent)
+            summed = add_slots(term_slots, clip_devices)
+            term_result[0] = jnp.sum(jnp.where(lane == 0, summed[:1], 0.0)) * scale
+            leaving.append(pltpu.make_async_copy(term_result, term_out, out_sems.at[2]))
+            leaving[-1].start()
+    for copy in leaving:
+        copy.wait()
     for sent in spec_sent + power_sent + [term_sent] + grad_sent:
         for copy in sent:
             copy.wait_send()
+
+
+def hand_on(mask_in, term_in, mask_out, term_out, sems):
+    copies = [
+        pltpu.make_async_copy(mask_in, mask_out, sems.at[0]),
+        pltpu.make_async_copy(term_in, term_out, sems.at[1]),
+    ]
+    for copy in copies:
+        copy.start()
+    for copy in copies:
+        copy.wait()
 
 
 def per_device(color_masks, source_weights, pupil_shifts, pupils, target_labels):
@@ -342,20 +364,19 @@
         shape = tables[name].shape[1:] if name in PER_SOURCE else tables[name].shape
         table_scratch.append(pltpu.VMEM(shape, bf16))
     far = pl.BlockSpec(memory_space=pltpu.HBM)
-    near = pl.BlockSpec(memory_space=pltpu.VMEM)
     dma = pltpu.SemaphoreType.DMA
     mask_grad, terms = pl.pallas_call(
         functools.partial(kernel, src_devices, clip_devices, scale),
         out_shape=(
             jax.ShapeDtypeStruct((2, rows, height), f32),
-            jax.ShapeDtypeStruct((8, LANES), f32),
+            jax.ShapeDtypeStruct((1,), f32),
         ),
         in_specs=[far] * (5 + len(ORDER)),
-        out_specs=(near, near),
+        out_specs=(far, far),
         scratch_shapes=table_scratch
         + [
             pltpu.SMEM((1, 2), jnp.int32),
-            pltpu.SMEM((1, 1), f32),
+            pltpu.SMEM((1,), f32),
             pltpu.VMEM((2, rows, height), f32),
             pltpu.VMEM(pupils.shape, f32),
             pltpu.VMEM((height, height), jnp.int32),
@@ -371,14 +392,26 @@
             dma((len(ORDER) + 5,)),
         ]
         + [dma((2, src_devices - 1))] * 6
-        + [dma((clip_devices - 1,))] * 2,
+        + [dma((clip_devices - 1,))] * 2
+        + [pltpu.VMEM((2, rows, height), f32), pltpu.SMEM((1,), f32), dma((3,))],
         compiler_params=pltpu.CompilerParams(
             collective_id=0, has_side_effects=True, vmem_limit_bytes=60 * 1024 * 1024
         ),
         name="abbe_gradient",
-    )(pupil_shifts, source_weights[None], masks_here, pupils, target_labels[0], *operands)
-    mask_grad = mask_grad - (4.0 * binarize) * (1.0 - masks_here * masks_here) * masks_here
-    return mask_grad[None], terms[0, :1]
+    )(pupil_shifts, source_weights, masks_here, pupils, target_labels[0], *operands)
+    mask_grad, terms = pl.pallas_call(
+        hand_on,
+        out_shape=(
+            jax.ShapeDtypeStruct((2, rows, height), f32),
+            jax.ShapeDtypeStruct((1,), f32),
+        ),
+        in_specs=[far, far],
+        out_specs=(far, far),
+        scratch_shapes=[dma((2,))],
+        compiler_params=pltpu.CompilerParams(vmem_limit_bytes=60 * 1024 * 1024),
+        name="hand_on",
+    )(mask_grad, terms)
+    return mask_grad[None], terms
 
 
 def solution(mesh):

time: 26.2 us -> 29.1 us (1.11)
  Pallas kernels: 21.9 us -> 27.6 us
  other arithmetic: 1.58 us -> 0 us
  local copies, waits for them, and re-layouts: 1.19 us -> 0 us
    pallas_call x0 -> x1, Pallas kernels: none -> 5.71 us  [per_device(): pl.pallas_call(hand_on, out_shape=(jax.ShapeDtypeStruct((2, rows, height)...]
    broadcast_in_dim x1 -> x0, other arithmetic: 1.58 us -> none  [per_device(): return (mask_grad[None], terms[0, :1])]
    slice x1 -> x0, local copies, waits for them, and re-layouts: 1.18 us -> none  [per_device(): return (mask_grad[None], terms[0, :1])]
where the time goes in v2:
time: 29.1 us; the launch traced here: 28.9 us
  Pallas kernels  27.6 us (95%)
  between operations  1.28 us (4%)
    pallas_call x1, Pallas kernels, per_device(): pl.pallas_call(functools.partial(kernel, src_devices, clip_devices, scale...  21.9 us
    pallas_call x1, Pallas kernels, per_device(): pl.pallas_call(hand_on, out_shape=(jax.ShapeDtypeStruct((2, rows, height)...  5.71 us

profile of v2, /device:TPU:0, one launch (start us, length us, event | category | flops | bytes accessed | tf_op | source)
XLA Modules:
  0.0 28.9 jit_solution(15985825642571827613)
XLA Ops:
  1.3 21.9 %abbe_gradient.1 = (f32[2,64,256]{2,1,0:T(8,128)}, f32[1]{0:T(128)}) custom-call(s32[1,2]{1,0:T(1,128)} %shifts_hbm.1, f32[1]{0:T(128)S(6)} %copy.19.weights_hbm, f32[2,64,256]{2,1,0:T(8,128)} %bitcast.4, f32[8,2,32,32]{3,2,1,0:T(8,128)} %pupils_hbm.1, s32[256,256]{1,0:T(8,128)} %bitcast.3, bf16[4,96,192]{2,1,0:T(8,128)(2,1)} %constant.24.clone.rest_0_, ...), custom_call_target="tpu_custom_call" | custom-call | tf_op jit(solution)/shard_map/abbe_gradient/pallas_call | solution.py:368
  23.2 5.7 %hand_on.1 = (f32[2,64,256]{2,1,0:T(8,128)}, f32[1]{0:T(128)}) custom-call(f32[2,64,256]{2,1,0:T(8,128)} %get-tuple-element.6.mask_in, f32[1]{0:T(128)} %get-tuple-element.7.term_in), custom_call_target="tpu_custom_call" | custom-call | tf_op jit(solution)/shard_map/hand_on/pallas_call | solution.py:402

commit v3 on v2

--- a/solution.py
+++ b/solution.py
@@ -143,6 +143,22 @@
     me = lax.axis_index("src")
     my_clip = lax.axis_index("clip")
 
+    def bring(name):
+        source = table_hbm[name]
+        if name in PER_SOURCE:
+            source = source.at[me]
+        return pltpu.make_async_copy(source, tables[name], local_sems.at[ORDER.index(name)])
+
+    copy_masks = pltpu.make_async_copy(masks_hbm, masks, local_sems.at[count])
+    copy_pupils = pltpu.make_async_copy(pupils_hbm, pupils, local_sems.at[count + 1])
+    copy_labels = pltpu.make_async_copy(labels_hbm, labels, local_sems.at[count + 2])
+    copy_shifts = pltpu.make_async_copy(shifts_hbm, shifts, local_sems.at[count + 3])
+    copy_weights = pltpu.make_async_copy(weights_hbm, weights, local_sems.at[count + 4])
+    copies = {name: bring(name) for name in ORDER}
+    copy_masks.start()
+    copies["row_in"].start()
+    copies["col_in"].start()
+
     barrier = pltpu.get_barrier_semaphore()
     for d in range(1, src_devices):
         pl.semaphore_signal(
@@ -154,21 +170,6 @@
             device_id_type=pl.DeviceIdType.MESH,
         )
 
-    def bring(name):
-        source = table_hbm[name]
-        if name in PER_SOURCE:
-            source = source.at[me]
-        return pltpu.make_async_copy(source, tables[name], local_sems.at[ORDER.index(name)])
-
-    copy_masks = pltpu.make_async_copy(masks_hbm, masks, local_sems.at[count])
-    copy_pupils = pltpu.make_async_copy(pupils_hbm, pupils, local_sems.at[count + 1])
-    copy_labels = pltpu.make_async_copy(labels_hbm, labels, local_sems.at[count + 2])
-    copy_shifts = pltpu.make_async_copy(shifts_hbm, shifts, local_sems.at[count + 3])
-    copy_weights = pltpu.make_async_copy(weights_hbm, weights, local_sems.at[count + 4])
-    copies = {name: bring(name) for name in ORDER}
-    copy_masks.start()
-    copies["row_in"].start()
-    copies["col_in"].start()
     copy_pupils.start()
     copy_shifts.start()
     copy_weights.start()
@@ -291,10 +292,6 @@
             thin.append(times_table(slope, tables["down_cols"][...]))
         slope = table_times(tables["down_rows"][...], jnp.concatenate(thin, axis=0))
         term = term + jnp.sum(slope * raw[k], axis=0, keepdims=True)
-        if k == 1:
-            term_slots[my_clip] = jnp.broadcast_to(0.5 * jnp.sum(term, axis=1, keepdims=True), (8, LANES))
-            term_sent = exchange("clip", clip_devices, my_clip, term_slots, term_send, term_recv)
-
         slope = slope * (weight * (2.0 / (channels * src_devices)))
         field_grad = fields[k] * jnp.concatenate([slope] * channels, axis=1)
         back = table_thrice(tables["field_back"][...], field_grad)
@@ -316,8 +313,15 @@
             exchange("src", src_devices, me, grad_slots.at[k], grad_send.at[k], grad_recv.at[k])
         )
 
+    term_slots[my_clip] = jnp.broadcast_to(0.5 * jnp.sum(term, axis=1, keepdims=True), (8, LANES))
+    term_sent = exchange("clip", clip_devices, my_clip, term_slots, term_send, term_recv)
+
     leaving = []
     for k in colors:
+        if k == 1:
+            for sent in spec_sent + power_sent + grad_sent[:1] + [term_sent]:
+                for copy in sent:
+                    copy.wait_send()
         arrive(grad_sent[k])
         spread = times_table(add_slots(grad_slots.at[k], src_devices), tables["col_back"][...])
         folded = jnp.concatenate([spread[:, :height], spread[:, height:]], axis=0)
@@ -332,21 +336,24 @@
             term_result[0] = jnp.sum(jnp.where(lane == 0, summed[:1], 0.0)) * scale
             leaving.append(pltpu.make_async_copy(term_result, term_out, out_sems.at[2]))
             leaving[-1].start()
+    for copy in grad_sent[1]:
+        copy.wait_send()
     for copy in leaving:
         copy.wait()
-    for sent in spec_sent + power_sent + [term_sent] + grad_sent:
-        for copy in sent:
-            copy.wait_send()
-
-
-def hand_on(mask_in, term_in, mask_out, term_out, sems):
-    copies = [
-        pltpu.make_async_copy(mask_in, mask_out, sems.at[0]),
-        pltpu.make_async_copy(term_in, term_out, sems.at[1]),
-    ]
-    for copy in copies:
+
+
+def hand_on(mask_in, term_in, mask_out, term_out, held, term_held, sems):
+    colors = range(mask_in.shape[0])
+    arriving = [pltpu.make_async_copy(mask_in.at[k], held.at[k], sems.at[k]) for k in colors]
+    leaving = [pltpu.make_async_copy(held.at[k], mask_out.at[k], sems.at[2 + k]) for k in colors]
+    arriving.append(pltpu.make_async_copy(term_in, term_held, sems.at[4]))
+    leaving.append(pltpu.make_async_copy(term_held, term_out, sems.at[5]))
+    for copy in arriving:
         copy.start()
-    for copy in copies:
+    for before, after in zip(arriving, leaving):
+        before.wait()
+        after.start()
+    for copy in leaving:
         copy.wait()
 
 
@@ -407,7 +414,7 @@
         ),
         in_specs=[far, far],
         out_specs=(far, far),
-        scratch_shapes=[dma((2,))],
+        scratch_shapes=[pltpu.VMEM((2, rows, height), f32), pltpu.SMEM((1,), f32), dma((6,))],
         compiler_params=pltpu.CompilerParams(vmem_limit_bytes=60 * 1024 * 1024),
         name="hand_on",
     )(mask_grad, terms)

time: 29.1 us -> 25.5 us (0.88)
  Pallas kernels: 27.6 us -> 24 us
    pallas_call x1, Pallas kernels: 5.71 us -> 2.18 us  [per_device(): pl.pallas_call(hand_on, out_shape=(jax.ShapeDtypeStruct((2, rows, height)...]
where the time goes in v3:
time: 25.5 us; the launch traced here: 25.3 us
  Pallas kernels  24 us (94%)
  between operations  1.28 us (5%)
    pallas_call x1, Pallas kernels, per_device(): pl.pallas_call(functools.partial(kernel, src_devices, clip_devices, scale...  21.8 us
    pallas_call x1, Pallas kernels, per_device(): pl.pallas_call(hand_on, out_shape=(jax.ShapeDtypeStruct((2, rows, height)...  2.18 us

profile of v3, /device:TPU:0, one launch (start us, length us, event | category | flops | bytes accessed | tf_op | source)
XLA Modules:
  0.0 25.3 jit_solution(7141108409983486595)
XLA Ops:
  1.3 21.8 %abbe_gradient.1 = (f32[2,64,256]{2,1,0:T(8,128)}, f32[1]{0:T(128)}) custom-call(s32[1,2]{1,0:T(1,128)} %shifts_hbm.1, f32[1]{0:T(128)S(6)} %copy.19.weights_hbm, f32[2,64,256]{2,1,0:T(8,128)} %bitcast.4, f32[8,2,32,32]{3,2,1,0:T(8,128)} %pupils_hbm.1, s32[256,256]{1,0:T(8,128)} %bitcast.3, bf16[4,96,192]{2,1,0:T(8,128)(2,1)} %constant.24.clone.rest_0_, ...), custom_call_target="tpu_custom_call" | custom-call | tf_op jit(solution)/shard_map/abbe_gradient/pallas_call | solution.py:375
  23.1 2.2 %hand_on.1 = (f32[2,64,256]{2,1,0:T(8,128)}, f32[1]{0:T(128)}) custom-call(f32[2,64,256]{2,1,0:T(8,128)} %get-tuple-element.6.mask_in, f32[1]{0:T(128)} %get-tuple-element.7.term_in), custom_call_target="tpu_custom_call" | custom-call | tf_op jit(solution)/shard_map/hand_on/pallas_call | solution.py:409

commit v4 on v3

--- a/solution.py
+++ b/solution.py
@@ -42,6 +42,20 @@
 def thrice(table):
     high, low = halves(table)
     return np.concatenate([high, low, high], axis=-1)
+
+
+def crossed(table):
+    high, low = halves(table)
+    return np.concatenate(
+        [np.concatenate([high, low], axis=1), np.concatenate([high, np.zeros_like(low)], axis=1)], axis=0
+    )
+
+
+def crossed_left(table):
+    high, low = halves(table)
+    return np.concatenate(
+        [np.concatenate([high, high], axis=1), np.concatenate([low, np.zeros_like(low)], axis=1)], axis=0
+    )
 
 
 def spaced(real, imag):
@@ -67,23 +81,24 @@
 
     both = np.concatenate([fc, fs], axis=0)
     row_in = np.stack([thrice(both[:, s * rows : (s + 1) * rows]) for s in range(src_devices)])
-    col_in = beside(np.concatenate([spaced(fc.T, fs.T), spaced(-fs.T, fc.T)], axis=0))
+    col_in = beside(spaced(fc.T, fs.T))
     half_in = np.zeros((LANES, LANES))
     half_in[:KP] = np.concatenate([bc.T, bs.T], axis=1)
     half_in[HALF : HALF + KP] = np.concatenate([-bs.T, bc.T], axis=1)
-    half_in = beside(half_in)
+    half_in = crossed(half_in)
     field_in = thrice(np.concatenate([bc, bs], axis=1))
     up_rows = thrice(up)
-    up_cols = beside(np.concatenate([up.T, np.zeros_like(up.T)], axis=0))
-    down_cols = beside(np.concatenate([up, up], axis=1))
+    high, low = halves(up.T)
+    up_cols = np.concatenate([high, high, low, np.zeros_like(low)], axis=0)
+    down_cols = crossed(up)
     down_rows = above(up.T)
     field_back = thrice(np.concatenate([bc.T, bs.T], axis=0))
-    half_back = beside(np.concatenate([spaced(bc, -bs), spaced(bs, bc)], axis=0))
-    col_back = np.zeros((LANES, 2 * height))
-    col_back[:K] = np.concatenate([fc, -fs], axis=1)
-    col_back[HALF : HALF + K] = np.concatenate([fs, fc], axis=1)
-    col_back = beside(col_back)
-    row_back = np.stack([above(both[:, s * rows : (s + 1) * rows].T) for s in range(src_devices)])
+    half_back = crossed(np.concatenate([spaced(bc, -bs), spaced(bs, bc)], axis=0))
+    col_back = np.zeros((LANES, height))
+    col_back[:K], col_back[HALF : HALF + K] = fc, fs
+    high, low = halves(col_back)
+    col_back = np.concatenate([high, high, low], axis=0)
+    row_back = np.stack([crossed_left(both[:, s * rows : (s + 1) * rows].T) for s in range(src_devices)])
     return dict(
         row_in=row_in, col_in=col_in, half_in=half_in, field_in=field_in, up_rows=up_rows, up_cols=up_cols,
         down_cols=down_cols, down_rows=down_rows, field_back=field_back, half_back=half_back,
@@ -107,18 +122,13 @@
     return high, (value - high.astype(f32)).astype(bf16)
 
 
-def times_table(value, table):
-    high, low = split(value)
-    width = table.shape[1] // 2
-    first = mm(high, table[:, :width]) + mm(high, table[:, width:])
-    return first + mm(low, table[:, :width])
-
-
-def table_times(table, value):
-    high, low = split(value)
-    height = table.shape[0] // 2
-    first = mm(table, high)
-    return first[:height] + first[height:] + mm(table[:height], low)
+def add_halves(value):
+    width = value.shape[1] // 2
+    return value[:, :width] + value[:, width:]
+
+
+def times_crossed(value, table):
+    return mm(jnp.concatenate(split(value), axis=1), table)
 
 
 def table_thrice(table, value):
@@ -216,8 +226,9 @@
     spec_sent, power_sent, grad_sent = [], [], []
     for k in colors:
         rows_done = table_thrice(tables["row_in"][...], masks[k])
-        stacked = jnp.concatenate([rows_done[:K], rows_done[K:]], axis=1)
-        spec_slots[k, me] = times_table(stacked, tables["col_in"][...])
+        pair = mm(jnp.concatenate(split(rows_done), axis=0), tables["col_in"][...])
+        done = pair[: 2 * K, :LANES] + pair[: 2 * K, LANES:] + pair[2 * K :, :LANES]
+        spec_slots[k, me] = done[:K] + rotate(done[K:])
         if k == 0:
             pl.semaphore_wait(barrier, src_devices + clip_devices - 2)
         spec_sent.append(
@@ -247,7 +258,7 @@
         window = pltpu.roll(total[k, pl.ds(first, KP), :], lax.rem(LANES - second, LANES), 1)
         turned = rotate(window)
         products = [pupil_real[c] * window + pupil_imag[c] * turned for c in range(channels)]
-        half = times_table(jnp.concatenate(products, axis=0), tables["half_in"][...])
+        half = add_halves(times_crossed(jnp.concatenate(products, axis=0), tables["half_in"][...]))
         half_high, half_low = split(half)
         turn_high, turn_low = split(rotate(half))
         columns = []
@@ -281,16 +292,26 @@
     for k in colors:
         arrive(power_sent[k])
         packed = add_slots(power_slots.at[k], src_devices)
-        coarse = jnp.concatenate([packed, pltpu.roll(packed, HALF, 1)], axis=0)
+        turned = pltpu.roll(packed, HALF, 1)
+        coarse = jnp.concatenate(
+            [jnp.where(low_half, packed, turned), jnp.where(low_half, turned, packed)], axis=0
+        )
         tall = table_thrice(tables["up_rows"][...], coarse)
         thin = []
         for r in range(0, height, CHUNK):
-            intensity = times_table(tall[r : r + CHUNK], tables["up_cols"][...])
+            part = tall[r : r + CHUNK]
+            high = part.astype(bf16)
+            wide_high = high.astype(f32)
+            mixed = jnp.where(low_half, wide_high, part - wide_high).astype(bf16)
+            intensity = mm(jnp.concatenate([mixed, high], axis=1), tables["up_cols"][...])
             level = jnp.tanh((0.5 * steepness) * (intensity - threshold))
             shifted = level + jnp.where(labels[r : r + CHUNK, :] == k + 1, -1.0, 1.0)
             slope = (0.25 * loss_weight * steepness) * shifted * (1.0 - level * level)
-            thin.append(times_table(slope, tables["down_cols"][...]))
-        slope = table_times(tables["down_rows"][...], jnp.concatenate(thin, axis=0))
+            thin.append(times_crossed(slope, tables["down_cols"][...]))
+        thin = jnp.concatenate(split(jnp.concatenate(thin, axis=0)), axis=1)
+        pair = mm(tables["down_rows"][...], thin)
+        slope = pair[:N, :LANES] + pair[N:, :LANES] + pair[:N, LANES:]
+        slope = slope + pltpu.roll(slope, HALF, 1)
         term = term + jnp.sum(slope * raw[k], axis=0, keepdims=True)
         slope = slope * (weight * (2.0 / (channels * src_devices)))
         field_grad = fields[k] * jnp.concatenate([slope] * channels, axis=1)
@@ -299,7 +320,7 @@
         for c in range(channels):
             block = back[:, c * LANES : (c + 1) * LANES]
             pieces.append(block[:KP] - rotate(block[KP:]))
-        product_grad = times_table(jnp.concatenate(pieces, axis=0), tables["half_back"][...])
+        product_grad = add_halves(times_crossed(jnp.concatenate(pieces, axis=0), tables["half_back"][...]))
         along = jnp.zeros((KP, LANES), f32)
         across = jnp.zeros((KP, LANES), f32)
         for c in range(channels):
@@ -323,11 +344,13 @@
                 for copy in sent:
                     copy.wait_send()
         arrive(grad_sent[k])
-        spread = times_table(add_slots(grad_slots.at[k], src_devices), tables["col_back"][...])
-        folded = jnp.concatenate([spread[:, :height], spread[:, height:]], axis=0)
+        gathered = add_slots(grad_slots.at[k], src_devices)
+        high, low = split(jnp.concatenate([gathered, -rotate(gathered)], axis=0))
+        folded = mm(jnp.concatenate([high, low, high], axis=1), tables["col_back"][...])
+        pair = mm(tables["row_back"][...], jnp.concatenate(split(folded), axis=0))
         plane = masks[k]
         pull = (4.0 * binarize) * (1.0 - plane * plane) * plane
-        result[k] = table_times(tables["row_back"][...], folded) - pull
+        result[k] = pair[: result.shape[1]] + pair[result.shape[1] :] - pull
         leaving.append(pltpu.make_async_copy(result.at[k], mask_out.at[k], out_sems.at[k]))
         leaving[-1].start()
         if k == 0:

time: 25.5 us -> 25.1 us (0.984)
  Pallas kernels: 24 us -> 23.6 us
    pallas_call x1, Pallas kernels: 21.8 us -> 21.4 us  [per_device(): pl.pallas_call(functools.partial(kernel, src_devices, clip_devices, scale...]
where the time goes in v4:
time: 25.1 us; the launch traced here: 24.9 us
  Pallas kernels  23.6 us (94%)
  between operations  1.28 us (5%)
    pallas_call x1, Pallas kernels, per_device(): pl.pallas_call(functools.partial(kernel, src_devices, clip_devices, scale...  21.4 us
    pallas_call x1, Pallas kernels, per_device(): pl.pallas_call(hand_on, out_shape=(jax.ShapeDtypeStruct((2, rows, height)...  2.18 us

profile of v4, /device:TPU:0, one launch (start us, length us, event | category | flops | bytes accessed | tf_op | source)
XLA Modules:
  0.0 24.9 jit_solution(13956477596368641183)
XLA Ops:
  1.3 21.4 %abbe_gradient.1 = (f32[2,64,256]{2,1,0:T(8,128)}, f32[1]{0:T(128)}) custom-call(s32[1,2]{1,0:T(1,128)} %shifts_hbm.1, f32[1]{0:T(128)S(6)} %copy.19.weights_hbm, f32[2,64,256]{2,1,0:T(8,128)} %bitcast.4, f32[8,2,32,32]{3,2,1,0:T(8,128)} %pupils_hbm.1, s32[256,256]{1,0:T(8,128)} %bitcast.3, bf16[4,96,192]{2,1,0:T(8,128)(2,1)} %constant.24.clone.rest_0_, ...), custom_call_target="tpu_custom_call" | custom-call | tf_op jit(solution)/shard_map/abbe_gradient/pallas_call | solution.py:398
  22.7 2.2 %hand_on.1 = (f32[2,64,256]{2,1,0:T(8,128)}, f32[1]{0:T(128)}) custom-call(f32[2,64,256]{2,1,0:T(8,128)} %get-tuple-element.6.mask_in, f32[1]{0:T(128)} %get-tuple-element.7.term_in), custom_call_target="tpu_custom_call" | custom-call | tf_op jit(solution)/shard_map/hand_on/pallas_call | solution.py:432

commit v5 on v4

--- a/solution.py
+++ b/solution.py
@@ -146,9 +146,9 @@
     tables = dict(zip(ORDER, rest[count + 2 : 2 * count + 2]))
     (
         shifts, weights, masks, pupils, labels, pupil_real, pupil_imag, fields, padded, total,
-        spec_slots, power_slots, grad_slots, term_slots,
-        local_sems, spec_send, spec_recv, power_send, power_recv,
-        grad_send, grad_recv, term_send, term_recv, result, term_result, out_sems,
+        spec_slots, shift_slots, weight_slots, shift_words, term_slots,
+        local_sems, spec_send, spec_recv, small_send, small_recv,
+        term_send, term_recv, result, term_result, out_sems,
     ) = rest[2 * count + 2 :]
     me = lax.axis_index("src")
     my_clip = lax.axis_index("clip")
@@ -218,12 +218,18 @@
     def rotate(value):
         return pltpu.roll(value, HALF, 1) * sign
 
+    copy_shifts.wait()
+    copy_weights.wait()
+    shift_slots[me] = jnp.broadcast_to(jnp.where(lane == 0, shifts[0, 0], shifts[0, 1]), (8, LANES))
+    weight_slots[me] = jnp.full((8, LANES), weights[0], f32)
+
     copy_masks.wait()
     copies["row_in"].wait()
     copies["col_in"].wait()
     height = masks.shape[2]
     colors = range(2)
-    spec_sent, power_sent, grad_sent = [], [], []
+    sources = range(src_devices)
+    spec_sent, small_sent = [], []
     for k in colors:
         rows_done = table_thrice(tables["row_in"][...], masks[k])
         pair = mm(jnp.concatenate(split(rows_done), axis=0), tables["col_in"][...])
@@ -234,6 +240,9 @@
         spec_sent.append(
             exchange("src", src_devices, me, spec_slots.at[k], spec_send.at[k], spec_recv.at[k])
         )
+        if k == 0:
+            small_sent = exchange("src", src_devices, me, shift_slots, small_send.at[0], small_recv.at[0])
+            small_sent += exchange("src", src_devices, me, weight_slots, small_send.at[1], small_recv.at[1])
 
     copy_pupils.wait()
     channels = pupils.shape[0]
@@ -243,45 +252,49 @@
         pupil_real[c] = jnp.concatenate([pr, blank, pr, blank], axis=1)
         pupil_imag[c] = jnp.concatenate([pi, blank, pi, blank], axis=1)
     padded[...] = jnp.zeros_like(padded)
-    copy_shifts.wait()
-    copy_weights.wait()
-    first = shifts[0, 0]
-    second = shifts[0, 1]
-    weight = weights[0]
+    arrive(small_sent)
+    copy_words = pltpu.make_async_copy(shift_slots, shift_words, local_sems.at[count + 5])
+    copy_words.start()
     copies["half_in"].wait()
     copies["field_in"].wait()
-
-    raw = []
+    copy_words.wait()
+    first = [shift_words[s, 0, 0] for s in sources]
+    second = [shift_words[s, 0, 1] for s in sources]
+    weight = [weight_slots[s, 0:1, :] for s in sources]
+
+    coarse, own = [], []
     for k in colors:
         arrive(spec_sent[k])
         total[k] = add_slots(spec_slots.at[k], src_devices)
-        window = pltpu.roll(total[k, pl.ds(first, KP), :], lax.rem(LANES - second, LANES), 1)
-        turned = rotate(window)
-        products = [pupil_real[c] * window + pupil_imag[c] * turned for c in range(channels)]
-        half = add_halves(times_crossed(jnp.concatenate(products, axis=0), tables["half_in"][...]))
-        half_high, half_low = split(half)
-        turn_high, turn_low = split(rotate(half))
-        columns = []
-        for c in range(channels):
-            rows = slice(c * KP, (c + 1) * KP)
-            columns.append(
-                jnp.concatenate(
-                    [half_high[rows], turn_high[rows], half_high[rows], turn_high[rows], half_low[rows], turn_low[rows]],
-                    axis=0,
+        summed_power = jnp.zeros((N, LANES), f32)
+        own_power = jnp.zeros((N, LANES), f32)
+        for s in sources:
+            window = pltpu.roll(total[k, pl.ds(first[s], KP), :], lax.rem(LANES - second[s], LANES), 1)
+            turned = rotate(window)
+            products = [pupil_real[c] * window + pupil_imag[c] * turned for c in range(channels)]
+            half = add_halves(times_crossed(jnp.concatenate(products, axis=0), tables["half_in"][...]))
+            half_high, half_low = split(half)
+            turn_high, turn_low = split(rotate(half))
+            columns = []
+            for c in range(channels):
+                rows = slice(c * KP, (c + 1) * KP)
+                columns.append(
+                    jnp.concatenate(
+                        [half_high[rows], turn_high[rows], half_high[rows], turn_high[rows], half_low[rows], turn_low[rows]],
+                        axis=0,
+                    )
                 )
-            )
-        wide = mm(tables["field_in"][...], jnp.concatenate(columns, axis=1))
-        fields[k] = wide
-        squares = wide * wide
-        summed = squares[:, :LANES]
-        for c in range(1, channels):
-            summed = summed + squares[:, c * LANES : (c + 1) * LANES]
-        power = (summed + pltpu.roll(summed, HALF, 1)) * (1.0 / (channels * src_devices))
-        raw.append(power)
-        power_slots[k, me] = jnp.where(low_half, power[: N // 2], power[N // 2 :]) * weight
-        power_sent.append(
-            exchange("src", src_devices, me, power_slots.at[k], power_send.at[k], power_recv.at[k])
-        )
+            wide = mm(tables["field_in"][...], jnp.concatenate(columns, axis=1))
+            fields[k, s] = wide
+            squares = wide * wide
+            summed = squares[:, :LANES]
+            for c in range(1, channels):
+                summed = summed + squares[:, c * LANES : (c + 1) * LANES]
+            power = (summed + pltpu.roll(summed, HALF, 1)) * (1.0 / (channels * src_devices))
+            summed_power = summed_power + power * weight[s]
+            own_power = own_power + jnp.where(me == s, power, 0.0)
+        coarse.append(summed_power)
+        own.append(own_power)
     copies["up_rows"].wait()
     copies["up_cols"].wait()
     copy_labels.wait()
@@ -289,14 +302,9 @@
         copies[name].wait()
 
     term = jnp.zeros((1, LANES), f32)
+    slopes = []
     for k in colors:
-        arrive(power_sent[k])
-        packed = add_slots(power_slots.at[k], src_devices)
-        turned = pltpu.roll(packed, HALF, 1)
-        coarse = jnp.concatenate(
-            [jnp.where(low_half, packed, turned), jnp.where(low_half, turned, packed)], axis=0
-        )
-        tall = table_thrice(tables["up_rows"][...], coarse)
+        tall = table_thrice(tables["up_rows"][...], coarse[k])
         thin = []
         for r in range(0, height, CHUNK):
             part = tall[r : r + CHUNK]
@@ -312,39 +320,33 @@
         pair = mm(tables["down_rows"][...], thin)
         slope = pair[:N, :LANES] + pair[N:, :LANES] + pair[:N, LANES:]
         slope = slope + pltpu.roll(slope, HALF, 1)
-        term = term + jnp.sum(slope * raw[k], axis=0, keepdims=True)
-        slope = slope * (weight * (2.0 / (channels * src_devices)))
-        field_grad = fields[k] * jnp.concatenate([slope] * channels, axis=1)
-        back = table_thrice(tables["field_back"][...], field_grad)
-        pieces = []
-        for c in range(channels):
-            block = back[:, c * LANES : (c + 1) * LANES]
-            pieces.append(block[:KP] - rotate(block[KP:]))
-        product_grad = add_halves(times_crossed(jnp.concatenate(pieces, axis=0), tables["half_back"][...]))
-        along = jnp.zeros((KP, LANES), f32)
-        across = jnp.zeros((KP, LANES), f32)
-        for c in range(channels):
-            block = product_grad[c * KP : (c + 1) * KP]
-            along = along + pupil_real[c] * block
-            across = across + pupil_imag[c] * block
-        window_grad = along - rotate(across)
-        padded[k, K - KP : K, :] = pltpu.roll(window_grad, second, 1)
-        grad_slots[k, me] = padded[k, pl.ds(K - KP - first, K), :]
-        grad_sent.append(
-            exchange("src", src_devices, me, grad_slots.at[k], grad_send.at[k], grad_recv.at[k])
-        )
-
+        term = term + jnp.sum(slope * own[k], axis=0, keepdims=True)
+        slopes.append(slope)
     term_slots[my_clip] = jnp.broadcast_to(0.5 * jnp.sum(term, axis=1, keepdims=True), (8, LANES))
     term_sent = exchange("clip", clip_devices, my_clip, term_slots, term_send, term_recv)
 
     leaving = []
     for k in colors:
-        if k == 1:
-            for sent in spec_sent + power_sent + grad_sent[:1] + [term_sent]:
-                for copy in sent:
-                    copy.wait_send()
-        arrive(grad_sent[k])
-        gathered = add_slots(grad_slots.at[k], src_devices)
+        gathered = jnp.zeros((K, LANES), f32)
+        for s in sources:
+            slope = slopes[k] * (weight[s] * (2.0 / (channels * src_devices)))
+            field_grad = fields[k, s] * jnp.concatenate([slope] * channels, axis=1)
+            back = table_thrice(tables["field_back"][...], field_grad)
+            pieces = []
+            for c in range(channels):
+                block = back[:, c * LANES : (c + 1) * LANES]
+                pieces.append(block[:KP] - rotate(block[KP:]))
+            product_grad = add_halves(times_crossed(jnp.concatenate(pieces, axis=0), tables["half_back"][...]))
+            along = jnp.zeros((KP, LANES), f32)
+            across = jnp.zeros((KP, LANES), f32)
+            for c in range(channels):
+                block = product_grad[c * KP : (c + 1) * KP]
+                along = along + pupil_real[c] * block
+                across = across + pupil_imag[c] * block
+            window_grad = along - rotate(across)
+            padded[k, s, K - KP : K, :] = pltpu.roll(window_grad, second[s], 1)
+            gathered = gathered + padded[k, s, pl.ds(K - KP - first[s], K), :]
+
         high, low = split(jnp.concatenate([gathered, -rotate(gathered)], axis=0))
         folded = mm(jnp.concatenate([high, low, high], axis=1), tables["col_back"][...])
         pair = mm(tables["row_back"][...], jnp.concatenate(split(folded), axis=0))
@@ -359,8 +361,9 @@
             term_result[0] = jnp.sum(jnp.where(lane == 0, summed[:1], 0.0)) * scale
             leaving.append(pltpu.make_async_copy(term_result, term_out, out_sems.at[2]))
             leaving[-1].start()
-    for copy in grad_sent[1]:
-        copy.wait_send()
+            for sent in spec_sent + [small_sent, term_sent]:
+                for copy in sent:
+                    copy.wait_send()
     for copy in leaving:
         copy.wait()
 
@@ -412,16 +415,17 @@
             pltpu.VMEM((height, height), jnp.int32),
             pltpu.VMEM((channels, KP, LANES), f32),
             pltpu.VMEM((channels, KP, LANES), f32),
-            pltpu.VMEM((2, N, channels * LANES), f32),
-            pltpu.VMEM((2, 2 * K - KP, LANES), f32),
+            pltpu.VMEM((2, src_devices, N, channels * LANES), f32),
+            pltpu.VMEM((2, src_devices, 2 * K - KP, LANES), f32),
             pltpu.VMEM((2, K, LANES), f32),
             pltpu.VMEM((2, src_devices, K, LANES), f32),
-            pltpu.VMEM((2, src_devices, N // 2, LANES), f32),
-            pltpu.VMEM((2, src_devices, K, LANES), f32),
+            pltpu.VMEM((src_devices, 8, LANES), jnp.int32),
+            pltpu.VMEM((src_devices, 8, LANES), f32),
+            pltpu.SMEM((src_devices, 8, LANES), jnp.int32),
             pltpu.VMEM((clip_devices, 8, LANES), f32),
-            dma((len(ORDER) + 5,)),
+            dma((len(ORDER) + 6,)),
         ]
-        + [dma((2, src_devices - 1))] * 6
+        + [dma((2, src_devices - 1))] * 4
         + [dma((clip_devices - 1,))] * 2
         + [pltpu.VMEM((2, rows, height), f32), pltpu.SMEM((1,), f32), dma((3,))],
         compiler_params=pltpu.CompilerParams(

time: 25.1 us -> 25.1 us (level)
  no operation moved by 1% of the time
where the time goes in v5:
time: 25.1 us; the launch traced here: 24.9 us
  Pallas kernels  23.6 us (94%)
  between operations  1.28 us (5%)
    pallas_call x1, Pallas kernels, per_device(): pl.pallas_call(functools.partial(kernel, src_devices, clip_devices, scale...  21.4 us
    pallas_call x1, Pallas kernels, per_device(): pl.pallas_call(hand_on, out_shape=(jax.ShapeDtypeStruct((2, rows, height)...  2.18 us

profile of v5, /device:TPU:0, one launch (start us, length us, event | category | flops | bytes accessed | tf_op | source)
XLA Modules:
  0.0 24.9 jit_solution(1925541752580984828)
XLA Ops:
  1.3 21.4 %abbe_gradient.1 = (f32[2,64,256]{2,1,0:T(8,128)}, f32[1]{0:T(128)}) custom-call(s32[1,2]{1,0:T(1,128)} %shifts_hbm.1, f32[1]{0:T(128)S(6)} %copy.19.weights_hbm, f32[2,64,256]{2,1,0:T(8,128)} %bitcast.4, f32[8,2,32,32]{3,2,1,0:T(8,128)} %pupils_hbm.1, s32[256,256]{1,0:T(8,128)} %bitcast.3, bf16[4,96,192]{2,1,0:T(8,128)(2,1)} %constant.24.clone.rest_0_, ...), custom_call_target="tpu_custom_call" | custom-call | tf_op jit(solution)/shard_map/abbe_gradient/pallas_call | solution.py:401
  22.7 2.2 %hand_on.1 = (f32[2,64,256]{2,1,0:T(8,128)}, f32[1]{0:T(128)}) custom-call(f32[2,64,256]{2,1,0:T(8,128)} %get-tuple-element.6.mask_in, f32[1]{0:T(128)} %get-tuple-element.7.term_in), custom_call_target="tpu_custom_call" | custom-call | tf_op jit(solution)/shard_map/hand_on/pallas_call | solution.py:436

commit v6 on v5

--- a/solution.py
+++ b/solution.py
@@ -56,6 +56,11 @@
     return np.concatenate(
         [np.concatenate([high, high], axis=1), np.concatenate([low, np.zeros_like(low)], axis=1)], axis=0
     )
+
+
+def stacked(table):
+    high, low = halves(table)
+    return np.concatenate([high, high, low], axis=0)
 
 
 def spaced(real, imag):
@@ -85,7 +90,7 @@
     half_in = np.zeros((LANES, LANES))
     half_in[:KP] = np.concatenate([bc.T, bs.T], axis=1)
     half_in[HALF : HALF + KP] = np.concatenate([-bs.T, bc.T], axis=1)
-    half_in = crossed(half_in)
+    half_in = stacked(np.concatenate([half_in, -half_in[:, HALF:], half_in[:, :HALF]], axis=1))
     field_in = thrice(np.concatenate([bc, bs], axis=1))
     up_rows = thrice(up)
     high, low = halves(up.T)
@@ -93,11 +98,10 @@
     down_cols = crossed(up)
     down_rows = above(up.T)
     field_back = thrice(np.concatenate([bc.T, bs.T], axis=0))
-    half_back = crossed(np.concatenate([spaced(bc, -bs), spaced(bs, bc)], axis=0))
+    half_back = stacked(np.concatenate([spaced(bc, -bs), spaced(bs, bc)], axis=0))
     col_back = np.zeros((LANES, height))
     col_back[:K], col_back[HALF : HALF + K] = fc, fs
-    high, low = halves(col_back)
-    col_back = np.concatenate([high, high, low], axis=0)
+    col_back = stacked(col_back)
     row_back = np.stack([crossed_left(both[:, s * rows : (s + 1) * rows].T) for s in range(src_devices)])
     return dict(
         row_in=row_in, col_in=col_in, half_in=half_in, field_in=field_in, up_rows=up_rows, up_cols=up_cols,
@@ -122,9 +126,9 @@
     return high, (value - high.astype(f32)).astype(bf16)
 
 
-def add_halves(value):
-    width = value.shape[1] // 2
-    return value[:, :width] + value[:, width:]
+def times_stacked(value, table):
+    high, low = split(value)
+    return mm(jnp.concatenate([high, low, high], axis=1), table)
 
 
 def times_crossed(value, table):
@@ -272,9 +276,9 @@
             window = pltpu.roll(total[k, pl.ds(first[s], KP), :], lax.rem(LANES - second[s], LANES), 1)
             turned = rotate(window)
             products = [pupil_real[c] * window + pupil_imag[c] * turned for c in range(channels)]
-            half = add_halves(times_crossed(jnp.concatenate(products, axis=0), tables["half_in"][...]))
-            half_high, half_low = split(half)
-            turn_high, turn_low = split(rotate(half))
+            both = times_stacked(jnp.concatenate(products, axis=0), tables["half_in"][...])
+            half_high, half_low = split(both[:, :LANES])
+            turn_high, turn_low = split(both[:, LANES:])
             columns = []
             for c in range(channels):
                 rows = slice(c * KP, (c + 1) * KP)
@@ -336,7 +340,7 @@
             for c in range(channels):
                 block = back[:, c * LANES : (c + 1) * LANES]
                 pieces.append(block[:KP] - rotate(block[KP:]))
-            product_grad = add_halves(times_crossed(jnp.concatenate(pieces, axis=0), tables["half_back"][...]))
+            product_grad = times_stacked(jnp.concatenate(pieces, axis=0), tables["half_back"][...])
             along = jnp.zeros((KP, LANES), f32)
             across = jnp.zeros((KP, LANES), f32)
             for c in range(channels):
@@ -347,8 +351,8 @@
             padded[k, s, K - KP : K, :] = pltpu.roll(window_grad, second[s], 1)
             gathered = gathered + padded[k, s, pl.ds(K - KP - first[s], K), :]
 
-        high, low = split(jnp.concatenate([gathered, -rotate(gathered)], axis=0))
-        folded = mm(jnp.concatenate([high, low, high], axis=1), tables["col_back"][...])
+        turned = jnp.concatenate([gathered, -rotate(gathered)], axis=0)
+        folded = times_stacked(turned, tables["col_back"][...])
         pair = mm(tables["row_back"][...], jnp.concatenate(split(folded), axis=0))
         plane = masks[k]
         pull = (4.0 * binarize) * (1.0 - plane * plane) * plane

time: 25.1 us -> 25.3 us (level)
  no operation moved by 1% of the time
where the time goes in v6:
time: 25.3 us; the launch traced here: 25.1 us
  Pallas kernels  23.8 us (94%)
  between operations  1.28 us (5%)
    pallas_call x1, Pallas kernels, per_device(): pl.pallas_call(functools.partial(kernel, src_devices, clip_devices, scale...  21.7 us
    pallas_call x1, Pallas kernels, per_device(): pl.pallas_call(hand_on, out_shape=(jax.ShapeDtypeStruct((2, rows, height)...  2.18 us

profile of v6, /device:TPU:0, one launch (start us, length us, event | category | flops | bytes accessed | tf_op | source)
XLA Modules:
  0.0 25.1 jit_solution(13531779561676813421)
XLA Ops:
  1.3 21.7 %abbe_gradient.1 = (f32[2,64,256]{2,1,0:T(8,128)}, f32[1]{0:T(128)}) custom-call(s32[1,2]{1,0:T(1,128)} %shifts_hbm.1, f32[1]{0:T(128)S(6)} %copy.19.weights_hbm, f32[2,64,256]{2,1,0:T(8,128)} %bitcast.4, f32[8,2,32,32]{3,2,1,0:T(8,128)} %pupils_hbm.1, s32[256,256]{1,0:T(8,128)} %bitcast.3, bf16[4,96,192]{2,1,0:T(8,128)(2,1)} %constant.24.clone.rest_0_, ...), custom_call_target="tpu_custom_call" | custom-call | tf_op jit(solution)/shard_map/abbe_gradient/pallas_call | solution.py:405
  22.9 2.2 %hand_on.1 = (f32[2,64,256]{2,1,0:T(8,128)}, f32[1]{0:T(128)}) custom-call(f32[2,64,256]{2,1,0:T(8,128)} %get-tuple-element.6.mask_in, f32[1]{0:T(128)} %get-tuple-element.7.term_in), custom_call_target="tpu_custom_call" | custom-call | tf_op jit(solution)/shard_map/hand_on/pallas_call | solution.py:440

commit v7 on v4

--- a/solution.py
+++ b/solution.py
@@ -153,6 +153,17 @@
     me = lax.axis_index("src")
     my_clip = lax.axis_index("clip")
 
+    barrier = pltpu.get_barrier_semaphore()
+    for d in range(1, src_devices):
+        pl.semaphore_signal(
+            barrier, inc=1, device_id={"src": lax.rem(me + d, src_devices)}, device_id_type=pl.DeviceIdType.MESH
+        )
+    for d in range(1, clip_devices):
+        pl.semaphore_signal(
+            barrier, inc=1, device_id={"clip": lax.rem(my_clip + d, clip_devices)},
+            device_id_type=pl.DeviceIdType.MESH,
+        )
+
     def bring(name):
         source = table_hbm[name]
         if name in PER_SOURCE:
@@ -168,17 +179,6 @@
     copy_masks.start()
     copies["row_in"].start()
     copies["col_in"].start()
-
-    barrier = pltpu.get_barrier_semaphore()
-    for d in range(1, src_devices):
-        pl.semaphore_signal(
-            barrier, inc=1, device_id={"src": lax.rem(me + d, src_devices)}, device_id_type=pl.DeviceIdType.MESH
-        )
-    for d in range(1, clip_devices):
-        pl.semaphore_signal(
-            barrier, inc=1, device_id={"clip": lax.rem(my_clip + d, clip_devices)},
-            device_id_type=pl.DeviceIdType.MESH,
-        )
 
     copy_pupils.start()
     copy_shifts.start()
@@ -313,6 +313,10 @@
         slope = pair[:N, :LANES] + pair[N:, :LANES] + pair[:N, LANES:]
         slope = slope + pltpu.roll(slope, HALF, 1)
         term = term + jnp.sum(slope * raw[k], axis=0, keepdims=True)
+        if k == 1:
+            term_slots[my_clip] = jnp.broadcast_to(0.5 * jnp.sum(term, axis=1, keepdims=True), (8, LANES))
+            term_sent = exchange("clip", clip_devices, my_clip, term_slots, term_send, term_recv)
+
         slope = slope * (weight * (2.0 / (channels * src_devices)))
         field_grad = fields[k] * jnp.concatenate([slope] * channels, axis=1)
         back = table_thrice(tables["field_back"][...], field_grad)
@@ -333,9 +337,6 @@
         grad_sent.append(
             exchange("src", src_devices, me, grad_slots.at[k], grad_send.at[k], grad_recv.at[k])
         )
-
-    term_slots[my_clip] = jnp.broadcast_to(0.5 * jnp.sum(term, axis=1, keepdims=True), (8, LANES))
-    term_sent = exchange("clip", clip_devices, my_clip, term_slots, term_send, term_recv)
 
     leaving = []
     for k in colors:

time: 25.1 us -> 25.1 us (level)
  no operation moved by 1% of the time
where the time goes in v7:
time: 25.1 us; the launch traced here: 24.9 us
  Pallas kernels  23.7 us (94%)
  between operations  1.28 us (5%)
    pallas_call x1, Pallas kernels, per_device(): pl.pallas_call(functools.partial(kernel, src_devices, clip_devices, scale...  21.5 us
    pallas_call x1, Pallas kernels, per_device(): pl.pallas_call(hand_on, out_shape=(jax.ShapeDtypeStruct((2, rows, height)...  2.18 us

profile of v7, /device:TPU:0, one launch (start us, length us, event | category | flops | bytes accessed | tf_op | source)
XLA Modules:
  0.0 24.9 jit_solution(17240384688166000514)
XLA Ops:
  1.3 21.5 %abbe_gradient.1 = (f32[2,64,256]{2,1,0:T(8,128)}, f32[1]{0:T(128)}) custom-call(s32[1,2]{1,0:T(1,128)} %shifts_hbm.1, f32[1]{0:T(128)S(6)} %copy.19.weights_hbm, f32[2,64,256]{2,1,0:T(8,128)} %bitcast.4, f32[8,2,32,32]{3,2,1,0:T(8,128)} %pupils_hbm.1, s32[256,256]{1,0:T(8,128)} %bitcast.3, bf16[4,96,192]{2,1,0:T(8,128)(2,1)} %constant.24.clone.rest_0_, ...), custom_call_target="tpu_custom_call" | custom-call | tf_op jit(solution)/shard_map/abbe_gradient/pallas_call | solution.py:399
  22.8 2.2 %hand_on.1 = (f32[2,64,256]{2,1,0:T(8,128)}, f32[1]{0:T(128)}) custom-call(f32[2,64,256]{2,1,0:T(8,128)} %get-tuple-element.6.mask_in, f32[1]{0:T(128)} %get-tuple-element.7.term_in), custom_call_target="tpu_custom_call" | custom-call | tf_op jit(solution)/shard_map/hand_on/pallas_call | solution.py:433

commit v8 on v7

--- a/solution.py
+++ b/solution.py
@@ -15,7 +15,7 @@
 N = 2 * KP
 LANES = 128
 HALF = 64
-CHUNK = 64
+CHUNK = 256
 
 steepness = 4.0
 threshold = 0.6

time: 25.1 us -> 24.9 us (level)
  Pallas kernels: 23.7 us -> 23.4 us
where the time goes in v8:
time: 24.9 us; the launch traced here: 24.7 us
  Pallas kernels  23.4 us (94%)
  between operations  1.28 us (5%)
    pallas_call x1, Pallas kernels, per_device(): pl.pallas_call(functools.partial(kernel, src_devices, clip_devices, scale...  21.2 us
    pallas_call x1, Pallas kernels, per_device(): pl.pallas_call(hand_on, out_shape=(jax.ShapeDtypeStruct((2, rows, height)...  2.18 us

profile of v8, /device:TPU:0, one launch (start us, length us, event | category | flops | bytes accessed | tf_op | source)
XLA Modules:
  0.0 24.7 jit_solution(13713225629818881785)
XLA Ops:
  1.3 21.2 %abbe_gradient.1 = (f32[2,64,256]{2,1,0:T(8,128)}, f32[1]{0:T(128)}) custom-call(s32[1,2]{1,0:T(1,128)} %shifts_hbm.1, f32[1]{0:T(128)S(6)} %copy.19.weights_hbm, f32[2,64,256]{2,1,0:T(8,128)} %bitcast.4, f32[8,2,32,32]{3,2,1,0:T(8,128)} %pupils_hbm.1, s32[256,256]{1,0:T(8,128)} %bitcast.3, bf16[4,96,192]{2,1,0:T(8,128)(2,1)} %constant.24.clone.rest_0_, ...), custom_call_target="tpu_custom_call" | custom-call | tf_op jit(solution)/shard_map/abbe_gradient/pallas_call | solution.py:399
  22.5 2.2 %hand_on.1 = (f32[2,64,256]{2,1,0:T(8,128)}, f32[1]{0:T(128)}) custom-call(f32[2,64,256]{2,1,0:T(8,128)} %get-tuple-element.6.mask_in, f32[1]{0:T(128)} %get-tuple-element.7.term_in), custom_call_target="tpu_custom_call" | custom-call | tf_op jit(solution)/shard_map/hand_on/pallas_call | solution.py:433
